TPU v7x, 128 devices: a whole 4x4x4 slice. The times are simulated.
128 devices in a mesh: fsdp: 64 (over x_lo, z, y, core), dp: 2 (over x_hi).
Axes of the slice: x: 4 (x_hi: 2, x_lo: 2; x = x_hi * 2 + x_lo), y: 4, z: 4, core: 2. Of those that a mesh axis runs over, the one named last changes fastest.
Arguments:
- queries: bfloat16 [256, 768], P(('fsdp', 'dp')), may hold values from -6 to 6
- w_proj: bfloat16 [768, 9216], P(None, 'fsdp'), may hold values from -0.21875 to 0.21875
- b_proj: bfloat16 [9216], P('fsdp'), may hold values from -3 to 3
- captions: bfloat16 [256, 9216], P(('fsdp', 'dp')), may hold values from -6 to 6
- ln_gain: float32 [9216], replicated, may hold values from 0.1 to 1.9
- ln_bias: float32 [9216], replicated, may hold values from -1.8 to 1.8
- fc1_weight: bfloat16 [9216, 36864], P(None, 'fsdp'), may hold values from -0.0625 to 0.0625
- fc1_bias: bfloat16 [36864], P('fsdp'), may hold values from -3 to 3
- fc2_weight: bfloat16 [36864, 9216], P('fsdp'), may hold values from -0.03125 to 0.03125
- fc2_bias: float32 [9216], replicated, may hold values from -1.8 to 1.8
- cotangent: bfloat16 [256, 9216], P(('fsdp', 'dp')), may hold values from -24 to 24
Outputs:
- out_queries: bfloat16 [256, 9216], P(('fsdp', 'dp'))
- out_captions: bfloat16 [256, 9216], P(('fsdp', 'dp'))
- grad_w_proj: float32 [768, 9216], P(None, 'fsdp')
- grad_b_proj: float32 [9216], P('fsdp')
All inputs are finite; a program needn't handle non-finite values.
Results may differ from a plain program's by a relative error of at most 0.017.
The roundings to bfloat16 on the way count: a program that leaves them out, or rounds other values in their place, can miss the bound.
Values may be sent and summed in bfloat16 or wider, within the bound.
No kernel may reach another device: no remote copies, remote signals or barrier semaphores. Data moves between devices by JAX's collectives and lax.ppermute only.
A program may use at most 192 MiB of HBM per device.

v0:
```python
import jax
import jax.numpy as jnp
from jax import lax
from jax.experimental import pallas as pl
from jax.experimental.pallas import tpu as pltpu
from jax.sharding import PartitionSpec as P

F32 = jnp.float32
BF16 = jnp.bfloat16
NX, NZ, NY, NC = 2, 4, 4, 2
LANES = 128


def pos(x, z, y, c):
    return ((x * NZ + z) * NY + y) * NC + c


def ring_pairs(along_z, shift):
    pairs = []
    for x in range(NX):
        for z in range(NZ):
            for y in range(NY):
                for c in range(NC):
                    if along_z[c]:
                        to = pos(x, (z + shift) % NZ, y, c)
                    else:
                        to = pos(x, z, (y + shift) % NY, c)
                    pairs.append((pos(x, z, y, c), to))
    return pairs


def swap_pairs(axis):
    pairs = []
    for x in range(NX):
        for z in range(NZ):
            for y in range(NY):
                for c in range(NC):
                    to = pos(1 - x, z, y, c) if axis == "x" else pos(x, z, y, 1 - c)
                    pairs.append((pos(x, z, y, c), to))
    return pairs


STAGE_A = (True, False)
STAGE_B = (False, True)


def send(value, pairs):
    return lax.ppermute(value, "fsdp", pairs)


def put(buffer, piece, index):
    return lax.dynamic_update_slice_in_dim(buffer, piece[None], index, 0)


def gather2(shard, axis, index):
    buffer = jnp.zeros((2,) + shard.shape, shard.dtype)
    buffer = put(buffer, shard, index)
    return put(buffer, send(shard, swap_pairs(axis)), 1 - index)


def gather4(shard, stage, index):
    got = [send(shard, ring_pairs(stage, k)) for k in (1, 2, 3)]
    buffer = jnp.zeros((4,) + shard.shape, shard.dtype)
    buffer = put(buffer, shard, index)
    for k in (1, 2, 3):
        buffer = put(buffer, got[k - 1], (index - k) % 4)
    return buffer


def take(blocks, index):
    return lax.dynamic_index_in_dim(blocks, index, 0, keepdims=False)


def scatter2(blocks, axis, index):
    got = send(take(blocks, 1 - index), swap_pairs(axis))
    return take(blocks, index).astype(F32) + got.astype(F32)


def scatter4(blocks, stage, index):
    got = [send(take(blocks, (index + k) % 4), ring_pairs(stage, k)) for k in (1, 2, 3)]
    total = take(blocks, index).astype(F32)
    for piece in got:
        total = total + piece.astype(F32)
    return total


CHUNK = 3072
PIECE = 16
SENT = [(0, 1), (1, 0)]


def row_stats(ref, width):
    rows = ref.shape[0]
    step = width // 8

    def total(of):
        def add(i, acc):
            for j in range(step // LANES):
                acc = acc + of(ref[:, pl.ds(pl.multiple_of(i * step, LANES) + j * LANES, LANES)].astype(F32))
            return acc

        acc = lax.fori_loop(0, 8, add, jnp.zeros((rows, LANES), F32))
        return jnp.sum(acc, axis=1, keepdims=True) / width

    centre = total(lambda v: v)
    inv_std = 1.0 / jnp.sqrt(total(lambda v: (v - centre) * (v - centre)) + 1e-05)
    return centre, inv_std


def chunk_of(i):
    return pl.ds(pl.multiple_of(i * CHUNK, CHUNK), CHUNK)


def at_piece(i):
    return pl.ds(pl.multiple_of(i * PIECE, PIECE), PIECE)


def own_rows(place, value):
    first = (place[1] * 2 + place[3]) * 2
    row = lax.broadcasted_iota(jnp.int32, value.shape, 0)
    return jnp.where((row == first) | (row == first + 1), value, 0.0)


def columns_copy(source, target, sems, i):
    cols = chunk_of(i)
    return pltpu.make_async_copy(source.at[:, cols], target.at[:, cols], sems.at[i])


def each_chunk(width, step):
    def run(i, carry):
        step(i, chunk_of(i))
        return carry

    lax.fori_loop(0, width // CHUNK, run, 0)


def token_block(place, i):
    c, ia, ib = place[0], place[1], place[2]
    k = i % 4
    if i < 4:
        return c * 4 + lax.rem(ib - k + 4, 4)
    return (1 - c) * 4 + lax.rem(ia - k + 4, 4)


NT = (((1,), (1,)), ((), ()))


def early_kernel(place, *refs):
    pieces, refs = refs[:2], refs[2:]
    (w2, gain, bias), refs = refs[:3], refs[3:]
    act, back, cot_own, cap, cot, back_t, w2v, sem, sem2 = refs
    width = cap.shape[1]
    lead = pieces[0].shape[1] - 2 * width
    copies = []
    for i in range(8):
        rows = pl.ds(i % 4 * PIECE, PIECE)
        near_rows = pieces[i // 4].at[rows, pl.ds(lead, width)]
        copies.append(pltpu.make_async_copy(near_rows, cap.at[pl.ds(i * PIECE, PIECE)], sem.at[i]))
    for copy in copies:
        copy.start()
    each_chunk(width, lambda i, cols: columns_copy(w2, w2v, sem2, i).start())
    for i in range(8):
        rows = pl.ds(i % 4 * PIECE, PIECE)
        near_rows = pieces[i // 4].at[rows, pl.ds(lead + width, width)]
        spot = at_piece(token_block(place, i))
        copies.append(pltpu.make_async_copy(near_rows, cot.at[spot], sem.at[8 + i]))
        copies[-1].start()
    for copy in copies[:8]:
        copy.wait()
    centre, inv_std = row_stats(cap, width)
    back_t[...] = jnp.zeros_like(back_t)
    for copy in copies[8:]:
        copy.wait()

    def step(i, cols):
        normed = (cap[:, cols].astype(F32) - centre) * inv_std
        act[:, cols] = (normed * gain[:, cols] + bias[:, cols]).astype(BF16)
        columns_copy(w2, w2v, sem2, i).wait()
        back_t[...] += lax.dot_general(w2v[:, cols], cot[:, cols], NT, preferred_element_type=F32)

    each_chunk(width, step)
    back[...] = back_t[...].T
    size = cot_own.shape[0]
    start = place[4] * size
    aligned = pl.multiple_of(start // LANES * LANES, LANES)
    near = cot[:, pl.ds(aligned, 2 * LANES)].astype(F32)
    near = pltpu.roll(near, lax.rem(2 * LANES - lax.rem(start, LANES), 2 * LANES), 1)
    cot_own[...] = near.T[:size]


def main_kernel(place, *refs):
    pieces, refs = refs[:2], refs[2:]
    (caps, act_c, back, w1, w2, gain, bias, b1, b2), refs = refs[:9], refs[9:]
    (kept, kept_far, sent, sent_far, stats), refs = refs[:5], refs[5:]
    proj_t, proj, acc, order, hidden, own_c, w1v, w2v, sem, sem1, sem2 = refs
    grad_t = proj_t
    width = proj.shape[1]
    tokens = proj.shape[0]
    size = width // 64
    c, ia, ib = place[0], place[1], place[2]

    def block_of(half, k, j, other_x):
        if half == 0:
            core, a, b = c, lax.rem(ia - j + 4, 4), lax.rem(ib - k + 4, 4)
        else:
            core, a, b = 1 - c, lax.rem(ib - j + 4, 4), lax.rem(ia - k + 4, 4)
        x = place[3] + other_x - 2 * place[3] * other_x
        z_y = jnp.where(core == 0, a * 8 + b * 2, b * 8 + a * 2)
        return pl.ds(pl.multiple_of((x * 32 + z_y + core) * size, PIECE), size)

    lead = caps.shape[1] - 2 * width
    own_rows_copy = pltpu.make_async_copy(caps.at[pl.ds(0, PIECE), pl.ds(lead, width)], own_c, sem.at[0])
    own_rows_copy.start()
    each_chunk(width, lambda i, cols: columns_copy(w1, w1v, sem1, i).start())
    for half in (0, 1):

        def bring_block(n, carry):
            source = pl.ds(pl.multiple_of(n * size, PIECE), size)
            proj_t[block_of(half, n // 8, n // 2 % 4, n % 2)] = pieces[half][source]
            return carry

        lax.fori_loop(0, 32, bring_block, 0, unroll=8)

    def turn(i, cols):
        proj[:, cols] = proj_t[cols].T

    each_chunk(width, turn)
    centre, inv_std = row_stats(proj, width)
    acc[...] = jnp.zeros_like(acc)

    def first(i, cols):
        normed = (proj[:, cols].astype(F32) - centre) * inv_std
        act = (normed * gain[:, cols] + bias[:, cols]).astype(BF16)
        act = jnp.concatenate([act_c[:, cols], act], axis=0)
        columns_copy(w1, w1v, sem1, i).wait()
        columns_copy(w2, w2v, sem2, i).start()
        acc[...] += lax.dot_general(w1v[:, cols], act, NT, preferred_element_type=F32)

    each_chunk(width, first)
    order[...] = jnp.maximum(acc[...].T + b1[...], 0.0).astype(BF16)
    grad_hidden = jnp.where(order[tokens:].astype(F32) > 0, back[...], 0.0).astype(BF16)

    def gradient(i, carry):
        cols = chunk_of(i)
        value = jnp.dot(grad_hidden, w1v[:, cols], preferred_element_type=F32)
        grad_t[cols] = value.astype(BF16).T
        normed = (proj[:, cols].astype(F32) - centre) * inv_std
        scaled = value * gain[:, cols]
        both = scaled * normed
        sum1, sum2 = carry
        for k in range(CHUNK // LANES):
            lanes = slice(k * LANES, (k + 1) * LANES)
            sum1, sum2 = sum1 + scaled[:, lanes], sum2 + both[:, lanes]
        return sum1, sum2

    zero = jnp.zeros((tokens, LANES), F32)
    sum1, sum2 = lax.fori_loop(0, width // CHUNK, gradient, (zero, zero))
    square = (tokens, tokens)

    def as_row(column):
        return jnp.broadcast_to(column, square).T[0:1]

    mean1 = as_row(jnp.sum(sum1, axis=1, keepdims=True) / width)
    mean2 = as_row(jnp.sum(sum2, axis=1, keepdims=True) / width)
    row = lax.broadcasted_iota(jnp.int32, (PIECE, tokens), 0)
    tail = jnp.where(row == 0, mean1, jnp.where(row == 1, mean2, 0.0)).astype(BF16)
    stats[...] = jnp.where(row < 8, as_row(centre), as_row(inv_std))
    tile_rows = 2 * PIECE
    grad_rows = 8 * (size + PIECE)
    piece_rows = grad_rows + width // LANES * tile_rows
    for half, first_k, out in ((1, 0, sent), (1, 1, sent_far), (0, 0, kept), (0, 1, kept_far)):

        def place_block(n, carry):
            k = n // 8
            base = pl.multiple_of(k * piece_rows + n % 8 * (size + PIECE), PIECE)
            out[pl.ds(base, size)] = grad_t[block_of(half, k + first_k, n // 2 % 4, n % 2)]
            out[pl.ds(base + size, PIECE)] = tail
            return carry

        lax.fori_loop(0, 24 if first_k else 8, place_block, 0, unroll=8)
    for i in range(8):
        base = 2 * i * PIECE
        hidden[base : base + PIECE] = order[i * PIECE : (i + 1) * PIECE]
        block = token_block(place, i)
        hidden[base + PIECE : base + 2 * PIECE] = order[at_piece(tokens // PIECE + block)]
    mine = at_piece(token_block(place, 0))
    own_rows_copy.wait()

    def second(i, cols):
        columns_copy(w2, w2v, sem2, i).wait()
        value = jnp.dot(hidden[...], w2v[:, cols], preferred_element_type=F32)
        first_c = value[:PIECE] + own_rows(place, own_c[:, cols].astype(F32) + b2[:, cols])
        first_q = value[PIECE : 2 * PIECE] + own_rows(place, proj[mine, cols].astype(F32) + b2[:, cols])
        value = jnp.concatenate([first_c, first_q, value[2 * PIECE :]], axis=0).astype(BF16)
        tiles = CHUNK // LANES
        for k in range(8):
            out = (kept, kept_far, sent, sent_far)[k // 4 * 2 + (k % 4 > 0)]
            base = max(k % 4 - 1, 0) * piece_rows + grad_rows + i * tiles * tile_rows
            for j in range(tiles):
                spot = pl.ds(pl.multiple_of(base + j * tile_rows, tile_rows), tile_rows)
                out[spot] = value[k * tile_rows : (k + 1) * tile_rows, j * LANES : (j + 1) * LANES]

    each_chunk(width, second)


def middle_kernel(place, *refs):
    sums, (own, *away), total = refs[:5], refs[6:10], refs[10]
    grad_rows = own.shape[1] // 14 * 5 * 8
    total[...] = sum(ref[grad_rows:].astype(F32) for ref in sums)
    ia, here = place[1], place[3]
    size = own.shape[1] // 14 * 5
    half = (own.shape[1] - size) // 2
    tile_rows = 2 * PIECE
    for j in range(4):
        out = own if j == 0 else away[j - 1]
        for other_x in range(2):
            a = lax.rem(ia - j + 4, 4)
            x = here + other_x - 2 * here * other_x
            spot = slice((j * 2 + other_x) * size, (j * 2 + other_x + 1) * size)
            out[other_x, :size] = sum(ref[spot].astype(F32) for ref in sums).astype(out.dtype)
            for kind in range(2):
                token = kind * PIECE + a * 4 + x * 2
                rows = [
                    total[pl.ds(token + r, half // 2, stride=tile_rows)] for r in range(2)
                ]
                base = size + kind * half
                out[other_x, base : base + half] = jnp.concatenate(rows, axis=0).astype(out.dtype)


ANY = pl.BlockSpec(memory_space=pl.ANY)
VMEM = pl.BlockSpec(memory_space=pltpu.VMEM)
SMEM = pl.BlockSpec(memory_space=pltpu.SMEM)


def call(kernel, ins, outs, scratch, limit, micros):
    return pl.pallas_call(
        kernel,
        in_specs=[spec for spec, _ in ins],
        out_specs=[spec for spec, _, _ in outs],
        out_shape=[jax.ShapeDtypeStruct(shape, dtype) for _, shape, dtype in outs],
        scratch_shapes=scratch,
        compiler_params=pltpu.CompilerParams(vmem_limit_bytes=limit * 1024 * 1024),
        cost_estimate=pl.CostEstimate(flops=0, bytes_accessed=micros * 3_690_000, transcendentals=0),
    )(*[value for _, value in ins])


def body(
    queries,
    w_proj,
    b_proj,
    captions,
    ln_gain,
    ln_bias,
    fc1_weight,
    fc1_bias,
    fc2_weight,
    fc2_bias,
    cotangent,
):
    where = lax.axis_index("fsdp")
    c = where % NC
    y = (where // NC) % NY
    z = (where // (NC * NY)) % NZ
    x = where // (NC * NY * NZ)
    ia = jnp.where(c == 0, z, y)
    ib = jnp.where(c == 0, y, z)
    place = jnp.stack([c, ia, ib, x, where]).astype(jnp.int32)
    rows, width = captions.shape
    qdim = queries.shape[1]
    cols = w_proj.shape[1]
    units = fc1_weight.shape[1]
    group = NX * NZ * NY * NC
    tokens = group * rows
    half = tokens // 2
    near = 8 * rows
    nw = rows * width // LANES

    def around(value, stage):
        return [value, *lax.optimization_barrier([send(value, ring_pairs(stage, k)) for k in (1, 2, 3)])]

    pack = jnp.concatenate([queries, captions, cotangent], axis=1)
    pack = gather2(pack, "x", x)
    pack = gather4(pack, STAGE_A, ia).reshape(near, -1)


    query_half = gather4(pack[:, :qdim], STAGE_B, ib).reshape(half, qdim)
    query_all = gather2(query_half, "core", c).reshape(tokens, qdim)
    other_query = lax.ppermute(query_all, "dp", SENT)
    proj_own = (
        lax.dot_general(w_proj, query_all, (((0,), (1,)), ((), ())), preferred_element_type=F32)
        + b_proj.astype(F32)[:, None]
    ).astype(BF16)
    pack = pack[:, qdim:]
    pack_pieces = [pack] + [send(pack, ring_pairs(STAGE_B, k)) for k in (1, 2)]

    pair = jnp.concatenate([proj_own, send(proj_own, swap_pairs("x"))], axis=0)
    plane = jnp.concatenate(around(pair, STAGE_A), axis=0)
    plane, pack = lax.optimization_barrier((plane, pack))
    pack_pieces.append(send(pack, ring_pairs(STAGE_B, 3)))
    planes = []
    for pieces in (pack_pieces, around(plane, STAGE_B)):
        own_plane = jnp.concatenate(pieces, axis=0)
        planes.append([own_plane, send(own_plane, swap_pairs("core"))])
    pack_planes, proj_planes = planes
    scratch = pltpu.VMEM
    dma = pltpu.SemaphoreType.DMA

    gain, bias = ln_gain[None, :], ln_bias[None, :]
    b1, b2 = fc1_bias.astype(F32)[None, :], fc2_bias[None, :]
    w1_t = fc1_weight.T
    size = cols + PIECE

    act_c, back, cot_own = call(
        early_kernel,
        [(SMEM, place)]
        + [(ANY, piece) for piece in pack_planes]
        + [(ANY, fc2_weight), (VMEM, gain), (VMEM, bias)],
        [(VMEM, (tokens, width), BF16), (VMEM, (tokens, units), F32), (VMEM, (cols, tokens), F32)],
        [
            scratch((tokens, width), BF16),
            scratch((tokens, width), BF16),
            scratch((units, tokens), F32),
            scratch((units, width), BF16),
            dma((16,)),
            dma((width // CHUNK,)),
        ],
        50,
        10,
    )

    grad_rows, out_rows = 8 * size, width // LANES * 2 * PIECE
    piece_rows = grad_rows + out_rows
    kept, kept_far, sent, sent_far, stats = call(
        main_kernel,
        [(SMEM, place)]
        + [(VMEM, piece) for piece in proj_planes]
        + [(ANY, pack_planes[0]), (VMEM, act_c), (VMEM, back), (ANY, w1_t), (ANY, fc2_weight)]
        + [(VMEM, gain), (VMEM, bias), (VMEM, b1), (VMEM, b2)],
        [(VMEM, (piece_rows, LANES), BF16), (VMEM, (3 * piece_rows, LANES), BF16)] * 2
        + [(VMEM, (PIECE, tokens), F32)],
        [
            scratch((width, tokens), BF16),
            scratch((tokens, width), BF16),
            scratch((units, 2 * tokens), F32),
            scratch((2 * tokens, units), BF16),
            scratch((2 * tokens, units), BF16),
            scratch((PIECE, width), BF16),
            scratch((units, width), BF16),
            scratch((units, width), BF16),
            dma((1,)),
            dma((width // CHUNK,)),
            dma((width // CHUNK,)),
        ],
        42,
        20,
    )

    total = (kept_far.astype(F32) + send(sent_far, swap_pairs("core")).astype(F32)).astype(BF16)
    got = [send(part, ring_pairs(STAGE_B, -1 - k)) for k, part in enumerate(total.reshape(3, piece_rows, LANES))]
    last = size + 2 * nw
    own, *away = call(
        middle_kernel,
        [(SMEM, place), (VMEM, kept), (VMEM, send(sent, swap_pairs("core")))]
        + [(VMEM, part) for part in got]
        + [(ANY, other_query)],
        [(VMEM, (2, last, LANES), F32)] + [(VMEM, (2, last, LANES), BF16)] * 3,
        [scratch((out_rows, LANES), F32)],
        16,
        3,
    )
    got = lax.optimization_barrier([send(away[k - 1], ring_pairs(STAGE_A, -k)) for k in (1, 2, 3)])
    total = own + sum(part.astype(F32) for part in got)
    total = total[0] + send(total[1].astype(BF16), swap_pairs("x")).astype(F32)
    grad_act, mean1, mean2 = total[:cols], total[cols : cols + 1], total[cols + 1 : cols + 2]
    part = lax.optimization_barrier(total[size:].astype(BF16))
    out_captions, out_queries = part[:nw].reshape(rows, width), part[nw:].reshape(rows, width)

    gain_own = lax.dynamic_slice_in_dim(ln_gain, where * cols, cols, 0)[:, None]
    centre, inv_std = stats[0:1], stats[8:9]
    normed_own = (proj_own.astype(F32) - centre) * inv_std
    scaled = grad_act * gain_own
    grad_input = (cot_own + inv_std * (scaled - mean1 - normed_own * mean2)).astype(BF16)
    other_input = lax.ppermute(grad_input, "dp", SENT)

    def terms(query_rows, grads):
        weight = lax.dot_general(
            query_rows, grads, (((0,), (1,)), ((), ())), preferred_element_type=F32
        )
        return weight, jnp.sum(grads.astype(F32), axis=1)

    weight0, bias0 = terms(query_all, grad_input)
    weight1, bias1 = terms(other_query, other_input)
    return out_queries, out_captions, weight0 + weight1, bias0 + bias1


def solution(mesh):
    placed = (
        P(("fsdp", "dp"), None),
        P(None, "fsdp"),
        P("fsdp"),
        P(("fsdp", "dp"), None),
        P(),
        P(),
        P(None, "fsdp"),
        P("fsdp"),
        P("fsdp", None),
        P(),
        P(("fsdp", "dp"), None),
    )
    return jax.shard_map(
        body,
        mesh=mesh,
        in_specs=placed,
        out_specs=(P(("fsdp", "dp"), None), P(("fsdp", "dp"), None), P(None, "fsdp"), P("fsdp")),
        check_vma=False,
    )
```

profile of v0, /device:TPU:6, one launch (start us, length us, event | category | flops | bytes accessed | tf_op | source)
XLA Modules:
  0.0 168.2 jit_solution(14089928645940400537)
XLA Ops:
  1.4 0.8 constant_dynamic-update-slice_fusion.1
  2.2 0.8 constant_dynamic-update-slice_fusion
  3.0 0.9 collective-permute-start
  4.9 2.5 %collective-permute-done = bf16[2,19200]{1,0:T(2,128)(2,1)S(1)} collective-permute-done((bf16[2,19200]{1,0:T(2,128)(2,1)S(1)}, bf16[2,19200]{1,0:T(2,128)(2,1)S(1)}, u32[]{:S(2)}, u32[]{:S(2)}) %collective-permute-start) | collective-permute-done | bytes 76832 | tf_op jit(solution)/shard_map/ppermute | solution.py:48
  7.5 2.0 %collective-permute-start.1 = (bf16[2,2,19200]{2,1,0:T(2,128)(2,1)S(1)}, bf16[2,2,19200]{2,1,0:T(2,128)(2,1)S(1)}, u32[]{:S(2)}, u32[]{:S(2)}) collective-permute-start(bf16[2,2,19200]{2,1,0:T(2,128)(2,1)S(1)} %bitcast_dynamic-update-slice_fusion.6), channel_id=1, source_target_pairs={{0,16},{2,6},{4,20},{6,10},{8,24},{10,14},{12,28},{14,2},{16,32},{... | collective-permute-start | bytes 460808 | tf_op jit(solution)/shard_map/ppermute | solution.py:48
  9.5 3.6 %collective-permute-start.2 = (bf16[2,2,19200]{2,1,0:T(2,128)(2,1)S(1)}, bf16[2,2,19200]{2,1,0:T(2,128)(2,1)S(1)}, u32[]{:S(2)}, u32[]{:S(2)}) collective-permute-start(bf16[2,2,19200]{2,1,0:T(2,128)(2,1)S(1)} %bitcast_dynamic-update-slice_fusion.6), channel_id=1, source_target_pairs={{0,32},{2,10},{4,36},{6,14},{8,40},{10,2},{12,44},{14,6},{16,48},{... | collective-permute-start | bytes 460808 | tf_op jit(solution)/shard_map/ppermute | solution.py:48
  13.1 1.0 collective-permute-start.3
  14.9 3.0 %collective-permute-done.2 = bf16[2,2,19200]{2,1,0:T(2,128)(2,1)S(1)} collective-permute-done((bf16[2,2,19200]{2,1,0:T(2,128)(2,1)S(1)}, bf16[2,2,19200]{2,1,0:T(2,128)(2,1)S(1)}, u32[]{:S(2)}, u32[]{:S(2)}) %collective-permute-start.2) | collective-permute-done | bytes 153632 | tf_op jit(solution)/shard_map/ppermute | solution.py:48
  18.7 1.6 collective-permute-start.4
  20.3 2.9 %collective-permute-start.5 = (bf16[16,768]{1,0:T(8,128)(2,1)S(1)}, bf16[16,768]{1,0:T(8,128)(2,1)S(1)}, u32[]{:S(2)}, u32[]{:S(2)}) collective-permute-start(bf16[16,768]{1,0:T(8,128)(2,1)S(1)} %slice.53), channel_id=1, source_target_pairs={{0,8},{2,34},{4,12},{6,38},{8,0},{10,42},{12,4},{14,46},{16,24},{1... | collective-permute-start | bytes 73736 | tf_op jit(solution)/shard_map/ppermute | solution.py:48
  23.2 1.3 collective-permute-start.6
  24.6 1.0 collective-permute-done.5
  25.7 1.4 collective-permute-done.6
  27.1 1.3 collective-permute-done.7
  28.6 0.9 collective-permute-start.8
  29.9 3.8 %collective-permute-start.17 = (bf16[16,18432]{1,0:T(8,128)(2,1)S(1)}, bf16[16,18432]{1,0:T(8,128)(2,1)S(1)}, u32[]{:S(2)}, u32[]{:S(2)}) collective-permute-start(bf16[16,18432]{1,0:T(8,128)(2,1)S(1)} %slice.54), channel_id=1, source_target_pairs={{0,8},{2,34},{4,12},{6,38},{8,0},{10,42},{12,4},{14,46},{16,24},{1... | collective-permute-start | bytes 1769480 | tf_op jit(solution)/shard_map/ppermute | solution.py:48
  33.7 2.2 %collective-permute-start.10 = (bf16[288,128]{1,0:T(8,128)(2,1)S(1)}, bf16[288,128]{1,0:T(8,128)(2,1)S(1)}, u32[]{:S(2)}, u32[]{:S(2)}) collective-permute-start(bf16[288,128]{1,0:T(8,128)(2,1)S(1)} %pad_maximum_fusion.1), channel_id=1, source_target_pairs={{0,32},{2,10},{4,36},{6,14},{8,40},{10,2},{12,44},{14,6},{16,48},{... | collective-permute-start | bytes 221192 | tf_op jit(solution)/shard_map/ppermute | solution.py:48
  35.9 1.7 collective-permute-start.11
  37.9 2.5 %collective-permute-done.10 = bf16[288,128]{1,0:T(8,128)(2,1)S(1)} collective-permute-done((bf16[288,128]{1,0:T(8,128)(2,1)S(1)}, bf16[288,128]{1,0:T(8,128)(2,1)S(1)}, u32[]{:S(2)}, u32[]{:S(2)}) %collective-permute-start.10) | collective-permute-done | bytes 73760 | tf_op jit(solution)/shard_map/ppermute | solution.py:48
  40.4 1.1 collective-permute-done.11
  41.6 7.1 %collective-permute-done.9 = bf16[288,128]{1,0:T(8,128)(2,1)S(1)} collective-permute-done((bf16[288,128]{1,0:T(8,128)(2,1)S(1)}, bf16[288,128]{1,0:T(8,128)(2,1)S(1)}, u32[]{:S(2)}, u32[]{:S(2)}) %collective-permute-start.9) | collective-permute-done | bytes 73760 | tf_op jit(solution)/shard_map/ppermute | solution.py:48
  48.7 2.3 %collective-permute-start.18 = (bf16[16,18432]{1,0:T(8,128)(2,1)S(1)}, bf16[16,18432]{1,0:T(8,128)(2,1)S(1)}, u32[]{:S(2)}, u32[]{:S(2)}) collective-permute-start(bf16[16,18432]{1,0:T(8,128)(2,1)S(1)} %slice.54), channel_id=1, source_target_pairs={{0,12},{2,50},{4,0},{6,54},{8,4},{10,58},{12,8},{14,62},{16,28},{1... | collective-permute-start | bytes 1769480 | tf_op jit(solution)/shard_map/ppermute | solution.py:48
  51.0 7.7 %collective-permute-done.18 = bf16[16,18432]{1,0:T(8,128)(2,1)S(1)} collective-permute-done((bf16[16,18432]{1,0:T(8,128)(2,1)S(1)}, bf16[16,18432]{1,0:T(8,128)(2,1)S(1)}, u32[]{:S(2)}, u32[]{:S(2)}) %collective-permute-start.18) | collective-permute-done | bytes 589856 | tf_op jit(solution)/shard_map/ppermute | solution.py:48
  59.3 4.6 %collective-permute-start.13 = (bf16[1152,128]{1,0:T(8,128)(2,1)S(1)}, bf16[1152,128]{1,0:T(8,128)(2,1)S(1)}, u32[]{:S(2)}, u32[]{:S(2)}) collective-permute-start(bf16[1152,128]{1,0:T(8,128)(2,1)S(1)} %constant_dynamic-update-slice_fusion.3), channel_id=1, source_target_pairs={{0,8},{2,34},{4,12},{6,38},{8,0},{10,42},{12,4},{14,46},{16,24},{1... | collective-permute-start | bytes 884744 | tf_op jit(solution)/shard_map/ppermute | solution.py:48
  64.0 0.7 constant_dynamic-update-slice_fusion.11
  64.7 2.5 %collective-permute-done.12 = bf16[1152,128]{1,0:T(8,128)(2,1)S(1)} collective-permute-done((bf16[1152,128]{1,0:T(8,128)(2,1)S(1)}, bf16[1152,128]{1,0:T(8,128)(2,1)S(1)}, u32[]{:S(2)}, u32[]{:S(2)}) %collective-permute-start.12) | collective-permute-done | bytes 294944 | tf_op jit(solution)/shard_map/ppermute | solution.py:48
  67.2 4.6 %collective-permute-done.13 = bf16[1152,128]{1,0:T(8,128)(2,1)S(1)} collective-permute-done((bf16[1152,128]{1,0:T(8,128)(2,1)S(1)}, bf16[1152,128]{1,0:T(8,128)(2,1)S(1)}, u32[]{:S(2)}, u32[]{:S(2)}) %collective-permute-start.13) | collective-permute-done | bytes 294944 | tf_op jit(solution)/shard_map/ppermute | solution.py:48
  72.5 0.7 constant_dynamic-update-slice_fusion.9
  74.1 10.5 %shard_map.138 = (bf16[128,9216]{1,0:T(8,128)(2,1)S(1)}, f32[128,576]{1,0:T(8,128)S(1)}, f32[144,128]{1,0:T(8,128)S(1)}) custom-call(s32[5]{0:T(128)S(1)} %stack.23.place, bf16[64,18432]{1,0:T(8,128)(2,1)} %copy-done.1, bf16[64,18432]{1,0:T(8,128)(2,1)} %collective-permute-done.19.refs_1_, bf16[576,9216]{1,0:T(8,128)(2,1)} %refs_6_.1, ...), custom_call_target="tpu_custom_call" | custom-call | bytes 36900000 | tf_op jit(solution)/shard_map/pallas_call | solution.py:336
  84.7 1.7 copy-done.2
  86.4 21.0 %shard_map.139 = (bf16[3584,128]{1,0:T(8,128)(2,1)S(1)}, bf16[10752,128]{1,0:T(8,128)(2,1)S(1)}, bf16[3584,128]{1,0:T(8,128)(2,1)S(1)}, bf16[10752,128]{1,0:T(8,128)(2,1)}, f32[16,128]{1,0:T(8,128)S(1)}) custom-call(s32[5]{0:T(128)S(1)} %stack.23.place, bf16[4608,128]{1,0:T(8,128)(2,1)} %constant_dynamic-update-slice_fusion.8.refs_0_, ...), custom_call_target="tpu_custom_call" | custom-call | bytes 73800000 | tf_op jit(solution)/shard_map/pallas_call | solution.py:336
  108.1 6.2 %collective-permute-done.21 = bf16[10752,128]{1,0:T(8,128)(2,1)S(1)} collective-permute-done((bf16[10752,128]{1,0:T(8,128)(2,1)}, bf16[10752,128]{1,0:T(8,128)(2,1)S(1)}, u32[]{:S(2)}, u32[]{:S(2)}) %collective-permute-start.21) | collective-permute-done | bytes 2752544 | tf_op jit(solution)/shard_map/ppermute | solution.py:48
  115.2 2.3 %collective-permute-start.22 = (bf16[3584,128]{1,0:T(8,128)(2,1)S(1)}, bf16[3584,128]{1,0:T(8,128)(2,1)S(1)}, u32[]{:S(2)}, u32[]{:S(2)}) collective-permute-start(bf16[3584,128]{1,0:T(8,128)(2,1)S(1)} %get-tuple-element.54), channel_id=1, source_target_pairs={{0,12},{2,50},{4,0},{6,54},{8,4},{10,58},{12,8},{14,62},{16,28},{1... | collective-permute-start | bytes 2752520 | tf_op jit(solution)/shard_map/ppermute | solution.py:48
  117.6 0.8 collective-permute-start.24
  118.4 1.4 collective-permute-start.25
  119.8 5.8 %collective-permute-done.25.refs_5_ = bf16[128,768]{1,0:T(8,128)(2,1)S(1)} collective-permute-done((bf16[128,768]{1,0:T(8,128)(2,1)S(1)}, bf16[128,768]{1,0:T(8,128)(2,1)S(1)}, u32[]{:S(2)}, u32[]{:S(2)}) %collective-permute-start.25) | collective-permute-done | bytes 196640 | tf_op jit(solution)/shard_map/ppermute | solution.py:388
  125.6 12.6 %collective-permute-done.22.refs_2_ = bf16[3584,128]{1,0:T(8,128)(2,1)S(1)} collective-permute-done((bf16[3584,128]{1,0:T(8,128)(2,1)S(1)}, bf16[3584,128]{1,0:T(8,128)(2,1)S(1)}, u32[]{:S(2)}, u32[]{:S(2)}) %collective-permute-start.22) | collective-permute-done | bytes 917536 | tf_op jit(solution)/shard_map/ppermute | solution.py:48
  138.2 3.8 %collective-permute-done.24.refs_4_ = bf16[3584,128]{1,0:T(8,128)(2,1)S(1)} collective-permute-done((bf16[3584,128]{1,0:T(8,128)(2,1)S(1)}, bf16[3584,128]{1,0:T(8,128)(2,1)S(1)}, u32[]{:S(2)}, u32[]{:S(2)}) %collective-permute-start.24) | collective-permute-done | bytes 917536 | tf_op jit(solution)/shard_map/ppermute | solution.py:48
  142.0 2.1 %shard_map.140 = (f32[2,448,128]{2,1,0:T(8,128)S(1)}, bf16[2,448,128]{2,1,0:T(8,128)(2,1)S(1)}, bf16[2,448,128]{2,1,0:T(8,128)(2,1)S(1)}, bf16[2,448,128]{2,1,0:T(8,128)(2,1)S(1)}) custom-call(s32[5]{0:T(128)S(1)} %stack.23.place, bf16[3584,128]{1,0:T(8,128)(2,1)S(1)} %get-tuple-element.37.refs_0_, bf16[3584,128]{1,0:T(8,128)(2,1)S(1)} %collective-permute-done.20.refs_1_, ...), custom_call_target="tpu_custom_call" | custom-call | bytes 11070000 | tf_op jit(solution)/shard_map/pallas_call | solution.py:336
  144.2 1.6 collective-permute-start.26
  145.8 0.9 collective-permute-start.28
  146.8 3.4 %collective-permute-done.26 = bf16[2,448,128]{2,1,0:T(8,128)(2,1)S(1)} collective-permute-done((bf16[2,448,128]{2,1,0:T(8,128)(2,1)S(1)}, bf16[2,448,128]{2,1,0:T(8,128)(2,1)S(1)}, u32[]{:S(2)}, u32[]{:S(2)}) %collective-permute-start.26) | collective-permute-done | bytes 229408 | tf_op jit(solution)/shard_map/ppermute | solution.py:48
  150.2 3.2 %collective-permute-done.27 = bf16[2,448,128]{2,1,0:T(8,128)(2,1)S(1)} collective-permute-done((bf16[2,448,128]{2,1,0:T(8,128)(2,1)S(1)}, bf16[2,448,128]{2,1,0:T(8,128)(2,1)S(1)}, u32[]{:S(2)}, u32[]{:S(2)}) %collective-permute-start.27) | collective-permute-done | bytes 229408 | tf_op jit(solution)/shard_map/ppermute | solution.py:48
  153.4 2.1 %collective-permute-done.28 = bf16[2,448,128]{2,1,0:T(8,128)(2,1)S(1)} collective-permute-done((bf16[2,448,128]{2,1,0:T(8,128)(2,1)S(1)}, bf16[2,448,128]{2,1,0:T(8,128)(2,1)S(1)}, u32[]{:S(2)}, u32[]{:S(2)}) %collective-permute-start.28) | collective-permute-done | bytes 229408 | tf_op jit(solution)/shard_map/ppermute | solution.py:48
  155.7 4.8 %collective-permute-done.29 = bf16[448,128]{1,0:T(8,128)(2,1)S(1)} collective-permute-done((bf16[448,128]{1,0:T(8,128)(2,1)S(1)}, bf16[448,128]{1,0:T(8,128)(2,1)S(1)}, u32[]{:S(2)}, u32[]{:S(2)}) %collective-permute-start.29) | collective-permute-done | bytes 114720 | tf_op jit(solution)/shard_map/ppermute | solution.py:48
  160.8 1.4 collective-permute-start.30
  163.5 2.8 %collective-permute-done.30 = bf16[144,128]{1,0:T(8,128)(2,1)S(1)} collective-permute-done((bf16[144,128]{1,0:T(8,128)(2,1)S(1)}, bf16[144,128]{1,0:T(8,128)(2,1)S(1)}, u32[]{:S(2)}, u32[]{:S(2)}) %collective-permute-start.30) | collective-permute-done | bytes 36896 | tf_op jit(solution)/shard_map/ppermute | solution.py:483
  166.5 1.0 convolution_add_fusion
  (84 shorter events, 10.9 us)
Async XLA Ops:
  0.6 27.7 %copy-start = (bf16[768,144]{0,1:T(8,128)(2,1)S(1)}, bf16[768,144]{0,1:T(8,128)(2,1)}, u32[]{:S(2)}) copy-start(bf16[768,144]{0,1:T(8,128)(2,1)} %param.12) | copy-start | bytes 663556
  3.0 4.5 %collective-permute-start = (bf16[2,19200]{1,0:T(2,128)(2,1)S(1)}, bf16[2,19200]{1,0:T(2,128)(2,1)S(1)}, u32[]{:S(2)}, u32[]{:S(2)}) collective-permute-start(bf16[2,19200]{1,0:T(2,128)(2,1)S(1)} %constant_dynamic-update-slice_fusion), channel_id=1, source_target_pairs={{0,64},{2,66},{4,68},{6,70},{8,72},{10,74},{12,76},{14,78},{16,80}... | collective-permute-start | bytes 230408 | tf_op jit(solution)/shard_map/ppermute | solution.py:48
  7.5 7.3 %collective-permute-start.1 = (bf16[2,2,19200]{2,1,0:T(2,128)(2,1)S(1)}, bf16[2,2,19200]{2,1,0:T(2,128)(2,1)S(1)}, u32[]{:S(2)}, u32[]{:S(2)}) collective-permute-start(bf16[2,2,19200]{2,1,0:T(2,128)(2,1)S(1)} %bitcast_dynamic-update-slice_fusion.6), channel_id=1, source_target_pairs={{0,16},{2,6},{4,20},{6,10},{8,24},{10,14},{12,28},{14,2},{16,32},{... | collective-permute-start | bytes 460808 | tf_op jit(solution)/shard_map/ppermute | solution.py:48
  9.5 8.4 %collective-permute-start.2 = (bf16[2,2,19200]{2,1,0:T(2,128)(2,1)S(1)}, bf16[2,2,19200]{2,1,0:T(2,128)(2,1)S(1)}, u32[]{:S(2)}, u32[]{:S(2)}) collective-permute-start(bf16[2,2,19200]{2,1,0:T(2,128)(2,1)S(1)} %bitcast_dynamic-update-slice_fusion.6), channel_id=1, source_target_pairs={{0,32},{2,10},{4,36},{6,14},{8,40},{10,2},{12,44},{14,6},{16,48},{... | collective-permute-start | bytes 460808 | tf_op jit(solution)/shard_map/ppermute | solution.py:48
  13.1 5.2 %collective-permute-start.3 = (bf16[2,2,19200]{2,1,0:T(2,128)(2,1)S(1)}, bf16[2,2,19200]{2,1,0:T(2,128)(2,1)S(1)}, u32[]{:S(2)}, u32[]{:S(2)}) collective-permute-start(bf16[2,2,19200]{2,1,0:T(2,128)(2,1)S(1)} %bitcast_dynamic-update-slice_fusion.6), channel_id=1, source_target_pairs={{0,48},{2,14},{4,52},{6,2},{8,56},{10,6},{12,60},{14,10},{16,0},{1... | collective-permute-start | bytes 460808 | tf_op jit(solution)/shard_map/ppermute | solution.py:48
  18.7 5.9 %collective-permute-start.4 = (bf16[16,768]{1,0:T(8,128)(2,1)S(1)}, bf16[16,768]{1,0:T(8,128)(2,1)S(1)}, u32[]{:S(2)}, u32[]{:S(2)}) collective-permute-start(bf16[16,768]{1,0:T(8,128)(2,1)S(1)} %slice.53), channel_id=1, source_target_pairs={{0,4},{2,18},{4,8},{6,22},{8,12},{10,26},{12,0},{14,30},{16,20},{1... | collective-permute-start | bytes 73736 | tf_op jit(solution)/shard_map/ppermute | solution.py:48
  20.3 5.3 %collective-permute-start.5 = (bf16[16,768]{1,0:T(8,128)(2,1)S(1)}, bf16[16,768]{1,0:T(8,128)(2,1)S(1)}, u32[]{:S(2)}, u32[]{:S(2)}) collective-permute-start(bf16[16,768]{1,0:T(8,128)(2,1)S(1)} %slice.53), channel_id=1, source_target_pairs={{0,8},{2,34},{4,12},{6,38},{8,0},{10,42},{12,4},{14,46},{16,24},{1... | collective-permute-start | bytes 73736 | tf_op jit(solution)/shard_map/ppermute | solution.py:48
  23.2 3.8 %collective-permute-start.6 = (bf16[16,768]{1,0:T(8,128)(2,1)S(1)}, bf16[16,768]{1,0:T(8,128)(2,1)S(1)}, u32[]{:S(2)}, u32[]{:S(2)}) collective-permute-start(bf16[16,768]{1,0:T(8,128)(2,1)S(1)} %slice.53), channel_id=1, source_target_pairs={{0,12},{2,50},{4,0},{6,54},{8,4},{10,58},{12,8},{14,62},{16,28},{1... | collective-permute-start | bytes 73736 | tf_op jit(solution)/shard_map/ppermute | solution.py:48
  27.0 1.3 collective-permute-start.7
  28.6 5.0 %collective-permute-start.8 = (bf16[144,128]{1,0:T(8,128)(2,1)S(1)}, bf16[144,128]{1,0:T(8,128)(2,1)S(1)}, u32[]{:S(2)}, u32[]{:S(2)}) collective-permute-start(bf16[144,128]{1,0:T(8,128)(2,1)S(1)} %get-tuple-element.62), channel_id=1, source_target_pairs={{0,64},{2,66},{4,68},{6,70},{8,72},{10,74},{12,76},{14,78},{16,80}... | collective-permute-start | bytes 110600 | tf_op jit(solution)/shard_map/ppermute | solution.py:48
  29.6 21.5 %collective-permute-start.16 = (bf16[16,18432]{1,0:T(8,128)(2,1)S(1)}, bf16[16,18432]{1,0:T(8,128)(2,1)S(1)}, u32[]{:S(2)}, u32[]{:S(2)}) collective-permute-start(bf16[16,18432]{1,0:T(8,128)(2,1)S(1)} %slice.54), channel_id=1, source_target_pairs={{0,4},{2,18},{4,8},{6,22},{8,12},{10,26},{12,0},{14,30},{16,20},{1... | collective-permute-start | bytes 1769480 | tf_op jit(solution)/shard_map/ppermute | solution.py:48
  29.9 21.1 %collective-permute-start.17 = (bf16[16,18432]{1,0:T(8,128)(2,1)S(1)}, bf16[16,18432]{1,0:T(8,128)(2,1)S(1)}, u32[]{:S(2)}, u32[]{:S(2)}) collective-permute-start(bf16[16,18432]{1,0:T(8,128)(2,1)S(1)} %slice.54), channel_id=1, source_target_pairs={{0,8},{2,34},{4,12},{6,38},{8,0},{10,42},{12,4},{14,46},{16,24},{1... | collective-permute-start | bytes 1769480 | tf_op jit(solution)/shard_map/ppermute | solution.py:48
  33.7 6.8 %collective-permute-start.10 = (bf16[288,128]{1,0:T(8,128)(2,1)S(1)}, bf16[288,128]{1,0:T(8,128)(2,1)S(1)}, u32[]{:S(2)}, u32[]{:S(2)}) collective-permute-start(bf16[288,128]{1,0:T(8,128)(2,1)S(1)} %pad_maximum_fusion.1), channel_id=1, source_target_pairs={{0,32},{2,10},{4,36},{6,14},{8,40},{10,2},{12,44},{14,6},{16,48},{... | collective-permute-start | bytes 221192 | tf_op jit(solution)/shard_map/ppermute | solution.py:48
  35.9 5.7 %collective-permute-start.11 = (bf16[288,128]{1,0:T(8,128)(2,1)S(1)}, bf16[288,128]{1,0:T(8,128)(2,1)S(1)}, u32[]{:S(2)}, u32[]{:S(2)}) collective-permute-start(bf16[288,128]{1,0:T(8,128)(2,1)S(1)} %pad_maximum_fusion.1), channel_id=1, source_target_pairs={{0,48},{2,14},{4,52},{6,2},{8,56},{10,6},{12,60},{14,10},{16,0},{1... | collective-permute-start | bytes 221192 | tf_op jit(solution)/shard_map/ppermute | solution.py:48
  37.5 11.1 %collective-permute-start.9 = (bf16[288,128]{1,0:T(8,128)(2,1)S(1)}, bf16[288,128]{1,0:T(8,128)(2,1)S(1)}, u32[]{:S(2)}, u32[]{:S(2)}) collective-permute-start(bf16[288,128]{1,0:T(8,128)(2,1)S(1)} %pad_maximum_fusion.1), channel_id=1, source_target_pairs={{0,16},{2,6},{4,20},{6,10},{8,24},{10,14},{12,28},{14,2},{16,32},{... | collective-permute-start | bytes 221192 | tf_op jit(solution)/shard_map/ppermute | solution.py:48
  48.7 10.0 %collective-permute-start.18 = (bf16[16,18432]{1,0:T(8,128)(2,1)S(1)}, bf16[16,18432]{1,0:T(8,128)(2,1)S(1)}, u32[]{:S(2)}, u32[]{:S(2)}) collective-permute-start(bf16[16,18432]{1,0:T(8,128)(2,1)S(1)} %slice.54), channel_id=1, source_target_pairs={{0,12},{2,50},{4,0},{6,54},{8,4},{10,58},{12,8},{14,62},{16,28},{1... | collective-permute-start | bytes 1769480 | tf_op jit(solution)/shard_map/ppermute | solution.py:48
  58.8 15.3 %copy-start.1 = (bf16[64,18432]{1,0:T(8,128)(2,1)}, bf16[64,18432]{1,0:T(8,128)(2,1)S(1)}, u32[]{:S(2)}) copy-start(bf16[64,18432]{1,0:T(8,128)(2,1)S(1)} %pad_maximum_fusion.refs_0_.refs_2_) | copy-start | bytes 7077892
  58.9 15.2 %copy-start.6 = (bf16[576]{0:T(1024)(128)(2,1)S(1)}, bf16[576]{0:T(1024)(128)(2,1)}, u32[]{:S(2)}) copy-start(bf16[576]{0:T(1024)(128)(2,1)} %param.18) | copy-start | bytes 3460
  58.9 15.2 %copy-start.3 = (f32[9216]{0:T(1024)S(1)}, f32[9216]{0:T(1024)}, u32[]{:S(2)}) copy-start(f32[9216]{0:T(1024)} %param.15) | copy-start | bytes 110596
  58.9 15.2 %copy-start.4 = (f32[9216]{0:T(1024)S(1)}, f32[9216]{0:T(1024)}, u32[]{:S(2)}) copy-start(f32[9216]{0:T(1024)} %param.16) | copy-start | bytes 110596
  58.9 15.2 %collective-permute-start.19 = (bf16[64,18432]{1,0:T(8,128)(2,1)S(1)}, bf16[64,18432]{1,0:T(8,128)(2,1)}, u32[]{:S(2)}, u32[]{:S(2)}) collective-permute-start(bf16[64,18432]{1,0:T(8,128)(2,1)S(1)} %pad_maximum_fusion.refs_0_.refs_2_), channel_id=1, source_target_pairs={{0,2},{2,0},{4,6},{6,4},{8,10},{10,8},{12,14},{14,12},{16,18},{18,... | collective-permute-start | bytes 7077896 | tf_op jit(solution)/shard_map/ppermute | solution.py:48
  59.0 8.2 %collective-permute-start.12 = (bf16[1152,128]{1,0:T(8,128)(2,1)S(1)}, bf16[1152,128]{1,0:T(8,128)(2,1)S(1)}, u32[]{:S(2)}, u32[]{:S(2)}) collective-permute-start(bf16[1152,128]{1,0:T(8,128)(2,1)S(1)} %constant_dynamic-update-slice_fusion.3), channel_id=1, source_target_pairs={{0,4},{2,18},{4,8},{6,22},{8,12},{10,26},{12,0},{14,30},{16,20},{1... | collective-permute-start | bytes 884744 | tf_op jit(solution)/shard_map/ppermute | solution.py:48
  59.3 12.5 %collective-permute-start.13 = (bf16[1152,128]{1,0:T(8,128)(2,1)S(1)}, bf16[1152,128]{1,0:T(8,128)(2,1)S(1)}, u32[]{:S(2)}, u32[]{:S(2)}) collective-permute-start(bf16[1152,128]{1,0:T(8,128)(2,1)S(1)} %constant_dynamic-update-slice_fusion.3), channel_id=1, source_target_pairs={{0,8},{2,34},{4,12},{6,38},{8,0},{10,42},{12,4},{14,46},{16,24},{1... | collective-permute-start | bytes 884744 | tf_op jit(solution)/shard_map/ppermute | solution.py:48
  64.0 7.9 %collective-permute-start.14 = (bf16[1152,128]{1,0:T(8,128)(2,1)S(1)}, bf16[1152,128]{1,0:T(8,128)(2,1)S(1)}, u32[]{:S(2)}, u32[]{:S(2)}) collective-permute-start(bf16[1152,128]{1,0:T(8,128)(2,1)S(1)} %constant_dynamic-update-slice_fusion.3), channel_id=1, source_target_pairs={{0,12},{2,50},{4,0},{6,54},{8,4},{10,58},{12,8},{14,62},{16,28},{1... | collective-permute-start | bytes 884744 | tf_op jit(solution)/shard_map/ppermute | solution.py:48
  74.0 10.7 %collective-permute-start.15 = (bf16[4608,128]{1,0:T(8,128)(2,1)}, bf16[4608,128]{1,0:T(8,128)(2,1)}, u32[]{:S(2)}, u32[]{:S(2)}) collective-permute-start(bf16[4608,128]{1,0:T(8,128)(2,1)} %constant_dynamic-update-slice_fusion.8.refs_0_), channel_id=1, source_target_pairs={{0,2},{2,0},{4,6},{6,4},{8,10},{10,8},{12,14},{14,12},{16,18},{18,... | collective-permute-start | bytes 3538952 | tf_op jit(solution)/shard_map/ppermute | solution.py:48
  74.1 10.6 %copy-start.5 = (f32[9216]{0:T(1024)S(1)}, f32[9216]{0:T(1024)}, u32[]{:S(2)}) copy-start(f32[9216]{0:T(1024)} %param.20) | copy-start | bytes 110596
  84.7 1.7 copy-start.2
  107.4 6.8 %collective-permute-start.21 = (bf16[10752,128]{1,0:T(8,128)(2,1)}, bf16[10752,128]{1,0:T(8,128)(2,1)S(1)}, u32[]{:S(2)}, u32[]{:S(2)}) collective-permute-start(bf16[10752,128]{1,0:T(8,128)(2,1)} %get-tuple-element.40), channel_id=1, source_target_pairs={{0,2},{2,0},{4,6},{6,4},{8,10},{10,8},{12,14},{14,12},{16,18},{18,... | collective-permute-start | bytes 8257544 | tf_op jit(solution)/shard_map/ppermute | solution.py:48
  108.0 17.6 %collective-permute-start.20 = (bf16[3584,128]{1,0:T(8,128)(2,1)S(1)}, bf16[3584,128]{1,0:T(8,128)(2,1)S(1)}, u32[]{:S(2)}, u32[]{:S(2)}) collective-permute-start(bf16[3584,128]{1,0:T(8,128)(2,1)S(1)} %get-tuple-element.38), channel_id=1, source_target_pairs={{0,2},{2,0},{4,6},{6,4},{8,10},{10,8},{12,14},{14,12},{16,18},{18,... | collective-permute-start | bytes 2752520 | tf_op jit(solution)/shard_map/ppermute | solution.py:48
  115.2 23.0 %collective-permute-start.22 = (bf16[3584,128]{1,0:T(8,128)(2,1)S(1)}, bf16[3584,128]{1,0:T(8,128)(2,1)S(1)}, u32[]{:S(2)}, u32[]{:S(2)}) collective-permute-start(bf16[3584,128]{1,0:T(8,128)(2,1)S(1)} %get-tuple-element.54), channel_id=1, source_target_pairs={{0,12},{2,50},{4,0},{6,54},{8,4},{10,58},{12,8},{14,62},{16,28},{1... | collective-permute-start | bytes 2752520 | tf_op jit(solution)/shard_map/ppermute | solution.py:48
  117.5 20.8 %collective-permute-start.23 = (bf16[3584,128]{1,0:T(8,128)(2,1)S(1)}, bf16[3584,128]{1,0:T(8,128)(2,1)S(1)}, u32[]{:S(2)}, u32[]{:S(2)}) collective-permute-start(bf16[3584,128]{1,0:T(8,128)(2,1)S(1)} %get-tuple-element.53), channel_id=1, source_target_pairs={{0,8},{2,34},{4,12},{6,38},{8,0},{10,42},{12,4},{14,46},{16,24},{1... | collective-permute-start | bytes 2752520 | tf_op jit(solution)/shard_map/ppermute | solution.py:48
  117.6 24.4 %collective-permute-start.24 = (bf16[3584,128]{1,0:T(8,128)(2,1)S(1)}, bf16[3584,128]{1,0:T(8,128)(2,1)S(1)}, u32[]{:S(2)}, u32[]{:S(2)}) collective-permute-start(bf16[3584,128]{1,0:T(8,128)(2,1)S(1)} %get-tuple-element.52), channel_id=1, source_target_pairs={{0,4},{2,18},{4,8},{6,22},{8,12},{10,26},{12,0},{14,30},{16,20},{1... | collective-permute-start | bytes 2752520 | tf_op jit(solution)/shard_map/ppermute | solution.py:48
  118.4 7.2 %collective-permute-start.25 = (bf16[128,768]{1,0:T(8,128)(2,1)S(1)}, bf16[128,768]{1,0:T(8,128)(2,1)S(1)}, u32[]{:S(2)}, u32[]{:S(2)}) collective-permute-start(bf16[128,768]{1,0:T(8,128)(2,1)S(1)} %bitcast.65), channel_id=1, source_target_pairs={{0,1},{1,0},{2,3},{3,2},{4,5},{5,4},{6,7},{7,6},{8,9},{9,8},{10,11... | collective-permute-start | bytes 589832 | tf_op jit(solution)/shard_map/ppermute | solution.py:388
  144.2 6.1 %collective-permute-start.26 = (bf16[2,448,128]{2,1,0:T(8,128)(2,1)S(1)}, bf16[2,448,128]{2,1,0:T(8,128)(2,1)S(1)}, u32[]{:S(2)}, u32[]{:S(2)}) collective-permute-start(bf16[2,448,128]{2,1,0:T(8,128)(2,1)S(1)} %get-tuple-element.42), channel_id=1, source_target_pairs={{0,48},{2,14},{4,52},{6,2},{8,56},{10,6},{12,60},{14,10},{16,0},{1... | collective-permute-start | bytes 688136 | tf_op jit(solution)/shard_map/ppermute | solution.py:48
  145.8 7.6 %collective-permute-start.27 = (bf16[2,448,128]{2,1,0:T(8,128)(2,1)S(1)}, bf16[2,448,128]{2,1,0:T(8,128)(2,1)S(1)}, u32[]{:S(2)}, u32[]{:S(2)}) collective-permute-start(bf16[2,448,128]{2,1,0:T(8,128)(2,1)S(1)} %get-tuple-element.43), channel_id=1, source_target_pairs={{0,32},{2,10},{4,36},{6,14},{8,40},{10,2},{12,44},{14,6},{16,48},{... | collective-permute-start | bytes 688136 | tf_op jit(solution)/shard_map/ppermute | solution.py:48
  145.8 9.7 %collective-permute-start.28 = (bf16[2,448,128]{2,1,0:T(8,128)(2,1)S(1)}, bf16[2,448,128]{2,1,0:T(8,128)(2,1)S(1)}, u32[]{:S(2)}, u32[]{:S(2)}) collective-permute-start(bf16[2,448,128]{2,1,0:T(8,128)(2,1)S(1)} %get-tuple-element.44), channel_id=1, source_target_pairs={{0,16},{2,6},{4,20},{6,10},{8,24},{10,14},{12,28},{14,2},{16,32},{... | collective-permute-start | bytes 688136 | tf_op jit(solution)/shard_map/ppermute | solution.py:48
  155.6 4.9 %collective-permute-start.29 = (bf16[448,128]{1,0:T(8,128)(2,1)S(1)}, bf16[448,128]{1,0:T(8,128)(2,1)S(1)}, u32[]{:S(2)}, u32[]{:S(2)}) collective-permute-start(bf16[448,128]{1,0:T(8,128)(2,1)S(1)} %fusion.3), channel_id=1, source_target_pairs={{0,64},{2,66},{4,68},{6,70},{8,72},{10,74},{12,76},{14,78},{16,80}... | collective-permute-start | bytes 344072 | tf_op jit(solution)/shard_map/ppermute | solution.py:48
  160.8 5.5 %collective-permute-start.30 = (bf16[144,128]{1,0:T(8,128)(2,1)S(1)}, bf16[144,128]{1,0:T(8,128)(2,1)S(1)}, u32[]{:S(2)}, u32[]{:S(2)}) collective-permute-start(bf16[144,128]{1,0:T(8,128)(2,1)S(1)} %get-tuple-element.51), channel_id=1, source_target_pairs={{0,1},{1,0},{2,3},{3,2},{4,5},{5,4},{6,7},{7,6},{8,9},{9,8},{10,11... | collective-permute-start | bytes 110600 | tf_op jit(solution)/shard_map/ppermute | solution.py:483
where the time goes:
time: 168 us
  waiting for transfers between devices  79.9 us (48%)
  starting transfers between devices  39.3 us (23%)
  Pallas kernels  33.7 us (20%)
  local copies, waits for them, and re-layouts  10.1 us (6%)
  other arithmetic  2.58 us (2%)
    ppermute x29, waiting for transfers between devices, send(): return lax.ppermute(value, 'fsdp', pairs)  71.3 us
    ppermute x29, starting transfers between devices, send(): return lax.ppermute(value, 'fsdp', pairs)  36.5 us
    pallas_call x3, Pallas kernels, call(): pl.pallas_call(kernel, in_specs=[spec for spec, _ in ins], out_specs=[spe...  33.7 us
    ppermute x1, waiting for transfers between devices, body(): other_query = lax.ppermute(query_all, 'dp', SENT)  5.8 us
    unnamed x22, local copies, waits for them, and re-layouts  5.48 us
  transfers between devices with their start and end apart: 31, of which 22 were waited for; matrix products, arithmetic and copies ran while one was open for 4% of the time, Pallas kernels for 6%

commit v1 on v0

--- a/solution.py
+++ b/solution.py
@@ -146,40 +146,33 @@
 
 
 def early_kernel(place, *refs):
-    pieces, refs = refs[:2], refs[2:]
-    (w2, gain, bias), refs = refs[:3], refs[3:]
-    act, back, cot_own, cap, cot, back_t, w2v, sem, sem2 = refs
+    pieces, refs = refs[:8], refs[8:]
+    gain, bias, act, cot, cot_own, own, cap, sem = refs
     width = cap.shape[1]
     lead = pieces[0].shape[1] - 2 * width
     copies = []
     for i in range(8):
-        rows = pl.ds(i % 4 * PIECE, PIECE)
-        near_rows = pieces[i // 4].at[rows, pl.ds(lead, width)]
+        near_rows = pieces[i].at[:, pl.ds(lead, width)]
         copies.append(pltpu.make_async_copy(near_rows, cap.at[pl.ds(i * PIECE, PIECE)], sem.at[i]))
     for copy in copies:
         copy.start()
-    each_chunk(width, lambda i, cols: columns_copy(w2, w2v, sem2, i).start())
     for i in range(8):
-        rows = pl.ds(i % 4 * PIECE, PIECE)
-        near_rows = pieces[i // 4].at[rows, pl.ds(lead + width, width)]
+        near_rows = pieces[i].at[:, pl.ds(lead + width, width)]
         spot = at_piece(token_block(place, i))
         copies.append(pltpu.make_async_copy(near_rows, cot.at[spot], sem.at[8 + i]))
         copies[-1].start()
     for copy in copies[:8]:
         copy.wait()
+    own[...] = cap[:PIECE]
     centre, inv_std = row_stats(cap, width)
-    back_t[...] = jnp.zeros_like(back_t)
-    for copy in copies[8:]:
-        copy.wait()
 
     def step(i, cols):
         normed = (cap[:, cols].astype(F32) - centre) * inv_std
         act[:, cols] = (normed * gain[:, cols] + bias[:, cols]).astype(BF16)
-        columns_copy(w2, w2v, sem2, i).wait()
-        back_t[...] += lax.dot_general(w2v[:, cols], cot[:, cols], NT, preferred_element_type=F32)
 
     each_chunk(width, step)
-    back[...] = back_t[...].T
+    for copy in copies[8:]:
+        copy.wait()
     size = cot_own.shape[0]
     start = place[4] * size
     aligned = pl.multiple_of(start // LANES * LANES, LANES)
@@ -189,10 +182,10 @@
 
 
 def main_kernel(place, *refs):
-    pieces, refs = refs[:2], refs[2:]
-    (caps, act_c, back, w1, w2, gain, bias, b1, b2), refs = refs[:9], refs[9:]
-    (kept, kept_far, sent, sent_far, stats), refs = refs[:5], refs[5:]
-    proj_t, proj, acc, order, hidden, own_c, w1v, w2v, sem, sem1, sem2 = refs
+    pieces, refs = refs[:8], refs[8:]
+    (own_c, act_c, cot, w1, w2, gain, bias, b1, b2), refs = refs[:9], refs[9:]
+    outs, stats, refs = refs[:8], refs[8], refs[9:]
+    proj_t, proj, acc, back_t, order, hidden, w1v, w2v, sem1, sem2 = refs
     grad_t = proj_t
     width = proj.shape[1]
     tokens = proj.shape[0]
@@ -208,18 +201,15 @@
         z_y = jnp.where(core == 0, a * 8 + b * 2, b * 8 + a * 2)
         return pl.ds(pl.multiple_of((x * 32 + z_y + core) * size, PIECE), size)
 
-    lead = caps.shape[1] - 2 * width
-    own_rows_copy = pltpu.make_async_copy(caps.at[pl.ds(0, PIECE), pl.ds(lead, width)], own_c, sem.at[0])
-    own_rows_copy.start()
     each_chunk(width, lambda i, cols: columns_copy(w1, w1v, sem1, i).start())
-    for half in (0, 1):
+    for i in range(8):
 
         def bring_block(n, carry):
             source = pl.ds(pl.multiple_of(n * size, PIECE), size)
-            proj_t[block_of(half, n // 8, n // 2 % 4, n % 2)] = pieces[half][source]
+            proj_t[block_of(i // 4, i % 4, n // 2, n % 2)] = pieces[i][source]
             return carry
 
-        lax.fori_loop(0, 32, bring_block, 0, unroll=8)
+        lax.fori_loop(0, 8, bring_block, 0, unroll=8)
 
     def turn(i, cols):
         proj[:, cols] = proj_t[cols].T
@@ -238,7 +228,14 @@
 
     each_chunk(width, first)
     order[...] = jnp.maximum(acc[...].T + b1[...], 0.0).astype(BF16)
-    grad_hidden = jnp.where(order[tokens:].astype(F32) > 0, back[...], 0.0).astype(BF16)
+    back_t[...] = jnp.zeros_like(back_t)
+
+    def backward(i, cols):
+        columns_copy(w2, w2v, sem2, i).wait()
+        back_t[...] += lax.dot_general(w2v[:, cols], cot[:, cols], NT, preferred_element_type=F32)
+
+    each_chunk(width, backward)
+    grad_hidden = jnp.where(order[tokens:].astype(F32) > 0, back_t[...].T, 0.0).astype(BF16)
 
     def gradient(i, carry):
         cols = chunk_of(i)
@@ -267,38 +264,33 @@
     stats[...] = jnp.where(row < 8, as_row(centre), as_row(inv_std))
     tile_rows = 2 * PIECE
     grad_rows = 8 * (size + PIECE)
-    piece_rows = grad_rows + width // LANES * tile_rows
-    for half, first_k, out in ((1, 0, sent), (1, 1, sent_far), (0, 0, kept), (0, 1, kept_far)):
+    for i in range(8):
 
         def place_block(n, carry):
-            k = n // 8
-            base = pl.multiple_of(k * piece_rows + n % 8 * (size + PIECE), PIECE)
-            out[pl.ds(base, size)] = grad_t[block_of(half, k + first_k, n // 2 % 4, n % 2)]
-            out[pl.ds(base + size, PIECE)] = tail
+            base = pl.multiple_of(n * (size + PIECE), PIECE)
+            outs[i][pl.ds(base, size)] = grad_t[block_of(i // 4, i % 4, n // 2, n % 2)]
+            outs[i][pl.ds(base + size, PIECE)] = tail
             return carry
 
-        lax.fori_loop(0, 24 if first_k else 8, place_block, 0, unroll=8)
+        lax.fori_loop(0, 8, place_block, 0, unroll=8)
     for i in range(8):
         base = 2 * i * PIECE
         hidden[base : base + PIECE] = order[i * PIECE : (i + 1) * PIECE]
         block = token_block(place, i)
         hidden[base + PIECE : base + 2 * PIECE] = order[at_piece(tokens // PIECE + block)]
     mine = at_piece(token_block(place, 0))
-    own_rows_copy.wait()
 
     def second(i, cols):
-        columns_copy(w2, w2v, sem2, i).wait()
         value = jnp.dot(hidden[...], w2v[:, cols], preferred_element_type=F32)
         first_c = value[:PIECE] + own_rows(place, own_c[:, cols].astype(F32) + b2[:, cols])
         first_q = value[PIECE : 2 * PIECE] + own_rows(place, proj[mine, cols].astype(F32) + b2[:, cols])
         value = jnp.concatenate([first_c, first_q, value[2 * PIECE :]], axis=0).astype(BF16)
         tiles = CHUNK // LANES
         for k in range(8):
-            out = (kept, kept_far, sent, sent_far)[k // 4 * 2 + (k % 4 > 0)]
-            base = max(k % 4 - 1, 0) * piece_rows + grad_rows + i * tiles * tile_rows
+            base = grad_rows + i * tiles * tile_rows
             for j in range(tiles):
                 spot = pl.ds(pl.multiple_of(base + j * tile_rows, tile_rows), tile_rows)
-                out[spot] = value[k * tile_rows : (k + 1) * tile_rows, j * LANES : (j + 1) * LANES]
+                outs[k][spot] = value[k * tile_rows : (k + 1) * tile_rows, j * LANES : (j + 1) * LANES]
 
     each_chunk(width, second)
 
@@ -383,25 +375,25 @@
     pack = gather4(pack, STAGE_A, ia).reshape(near, -1)
 
 
-    query_half = gather4(pack[:, :qdim], STAGE_B, ib).reshape(half, qdim)
-    query_all = gather2(query_half, "core", c).reshape(tokens, qdim)
+    def both_cores(pieces):
+        return pieces + [send(piece, swap_pairs("core")) for piece in pieces]
+
+    pack_pieces = around(pack, STAGE_B)
+    query_half = jnp.zeros((4, near, qdim), BF16)
+    for k in range(4):
+        query_half = put(query_half, pack_pieces[k][:, :qdim], (ib - k) % 4)
+    query_all = gather2(query_half.reshape(half, qdim), "core", c).reshape(tokens, qdim)
     other_query = lax.ppermute(query_all, "dp", SENT)
     proj_own = (
         lax.dot_general(w_proj, query_all, (((0,), (1,)), ((), ())), preferred_element_type=F32)
         + b_proj.astype(F32)[:, None]
     ).astype(BF16)
-    pack = pack[:, qdim:]
-    pack_pieces = [pack] + [send(pack, ring_pairs(STAGE_B, k)) for k in (1, 2)]
+    pack_pieces = both_cores(pack_pieces)
 
     pair = jnp.concatenate([proj_own, send(proj_own, swap_pairs("x"))], axis=0)
+    pair, pack_pieces = lax.optimization_barrier((pair, pack_pieces))
     plane = jnp.concatenate(around(pair, STAGE_A), axis=0)
-    plane, pack = lax.optimization_barrier((plane, pack))
-    pack_pieces.append(send(pack, ring_pairs(STAGE_B, 3)))
-    planes = []
-    for pieces in (pack_pieces, around(plane, STAGE_B)):
-        own_plane = jnp.concatenate(pieces, axis=0)
-        planes.append([own_plane, send(own_plane, swap_pairs("core"))])
-    pack_planes, proj_planes = planes
+    proj_pieces = both_cores(around(plane, STAGE_B))
     scratch = pltpu.VMEM
     dma = pltpu.SemaphoreType.DMA
 
@@ -410,58 +402,54 @@
     w1_t = fc1_weight.T
     size = cols + PIECE
 
-    act_c, back, cot_own = call(
+    act_c, cot, cot_own, own_c = call(
         early_kernel,
         [(SMEM, place)]
-        + [(ANY, piece) for piece in pack_planes]
-        + [(ANY, fc2_weight), (VMEM, gain), (VMEM, bias)],
-        [(VMEM, (tokens, width), BF16), (VMEM, (tokens, units), F32), (VMEM, (cols, tokens), F32)],
-        [
-            scratch((tokens, width), BF16),
-            scratch((tokens, width), BF16),
-            scratch((units, tokens), F32),
-            scratch((units, width), BF16),
-            dma((16,)),
-            dma((width // CHUNK,)),
-        ],
-        50,
-        10,
+        + [(VMEM, piece) for piece in pack_pieces]
+        + [(VMEM, gain), (VMEM, bias)],
+        [(VMEM, (tokens, width), BF16)] * 2 + [(VMEM, (cols, tokens), F32), (VMEM, (PIECE, width), BF16)],
+        [scratch((tokens, width), BF16), dma((16,))],
+        16,
+        5,
     )
 
     grad_rows, out_rows = 8 * size, width // LANES * 2 * PIECE
     piece_rows = grad_rows + out_rows
-    kept, kept_far, sent, sent_far, stats = call(
+    *parts, stats = call(
         main_kernel,
         [(SMEM, place)]
-        + [(VMEM, piece) for piece in proj_planes]
-        + [(ANY, pack_planes[0]), (VMEM, act_c), (VMEM, back), (ANY, w1_t), (ANY, fc2_weight)]
+        + [(VMEM, piece) for piece in proj_pieces]
+        + [(VMEM, own_c), (VMEM, act_c), (VMEM, cot), (ANY, w1_t), (ANY, fc2_weight)]
         + [(VMEM, gain), (VMEM, bias), (VMEM, b1), (VMEM, b2)],
-        [(VMEM, (piece_rows, LANES), BF16), (VMEM, (3 * piece_rows, LANES), BF16)] * 2
-        + [(VMEM, (PIECE, tokens), F32)],
+        [(VMEM, (piece_rows, LANES), BF16)] * 8 + [(VMEM, (PIECE, tokens), F32)],
         [
             scratch((width, tokens), BF16),
             scratch((tokens, width), BF16),
             scratch((units, 2 * tokens), F32),
+            scratch((units, tokens), F32),
             scratch((2 * tokens, units), BF16),
             scratch((2 * tokens, units), BF16),
-            scratch((PIECE, width), BF16),
             scratch((units, width), BF16),
             scratch((units, width), BF16),
-            dma((1,)),
             dma((width // CHUNK,)),
             dma((width // CHUNK,)),
         ],
-        42,
+        36,
         20,
     )
 
-    total = (kept_far.astype(F32) + send(sent_far, swap_pairs("core")).astype(F32)).astype(BF16)
-    got = [send(part, ring_pairs(STAGE_B, -1 - k)) for k, part in enumerate(total.reshape(3, piece_rows, LANES))]
+    got = []
+    for k in (2, 1, 3, 0):
+        part = send(parts[4 + k], swap_pairs("core"))
+        if k:
+            part = (parts[k].astype(F32) + part.astype(F32)).astype(BF16)
+            part = send(part, ring_pairs(STAGE_B, -k))
+        got.append(part)
     last = size + 2 * nw
     own, *away = call(
         middle_kernel,
-        [(SMEM, place), (VMEM, kept), (VMEM, send(sent, swap_pairs("core")))]
-        + [(VMEM, part) for part in got]
+        [(SMEM, place)]
+        + [(VMEM, part) for part in (parts[0], *got)]
         + [(ANY, other_query)],
         [(VMEM, (2, last, LANES), F32)] + [(VMEM, (2, last, LANES), BF16)] * 3,
         [scratch((out_rows, LANES), F32)],

time: 168 us -> 156 us (0.929)
  waiting for transfers between devices: 79.9 us -> 71.5 us
  Pallas kernels: 33.7 us -> 26.9 us
  local copies, waits for them, and re-layouts: 10.1 us -> 13.5 us
    ppermute x29 -> x34, waiting for transfers between devices: 71.3 us -> 62.6 us  [send(): return lax.ppermute(value, 'fsdp', pairs)]
    pallas_call x3, Pallas kernels: 33.7 us -> 26.9 us  [call(): pl.pallas_call(kernel, in_specs=[spec for spec, _ in ins], out_specs=[spe...]
    unnamed x22 -> x33, local copies, waits for them, and re-layouts: 5.48 us -> 9.21 us
    ppermute x29 -> x34, starting transfers between devices: 36.5 us -> 36.9 us  [send(): return lax.ppermute(value, 'fsdp', pairs)]
  transfers between devices with their start and end apart: 31 -> 36, of which waited for: 22 -> 24; matrix products, arithmetic and copies ran while one was open for 4% -> 3% of each run, Pallas kernels for 6% -> 3%
where the time goes in v1:
time: 156 us; the launch traced here: 155 us
  waiting for transfers between devices  71.5 us (46%)
  starting transfers between devices  39.4 us (25%)
  Pallas kernels  26.9 us (17%)
  local copies, waits for them, and re-layouts  13.5 us (9%)
  other arithmetic  1.74 us (1%)
    ppermute x34, waiting for transfers between devices, send(): return lax.ppermute(value, 'fsdp', pairs)  62.6 us
    ppermute x34, starting transfers between devices, send(): return lax.ppermute(value, 'fsdp', pairs)  36.9 us
    pallas_call x3, Pallas kernels, call(): pl.pallas_call(kernel, in_specs=[spec for spec, _ in ins], out_specs=[spe...  26.9 us
    unnamed x33, local copies, waits for them, and re-layouts  9.21 us
    ppermute x1, waiting for transfers between devices, body(): other_query = lax.ppermute(query_all, 'dp', SENT)  5.76 us
    ppermute x1, waiting for transfers between devices, body(): other_input = lax.ppermute(grad_input, 'dp', SENT)  3.18 us
  transfers between devices with their start and end apart: 36, of which 24 were waited for; matrix products, arithmetic and copies ran while one was open for 3% of the time, Pallas kernels for 3%

profile of v1, /device:TPU:6, one launch (start us, length us, event | category | flops | bytes accessed | tf_op | source)
XLA Modules:
  0.0 155.5 jit_solution(1245792358573667569)
XLA Ops:
  3.0 0.9 collective-permute-start
  4.2 3.3 %collective-permute-done = bf16[2,19200]{1,0:T(2,128)(2,1)S(1)} collective-permute-done((bf16[2,19200]{1,0:T(2,128)(2,1)S(1)}, bf16[2,19200]{1,0:T(2,128)(2,1)S(1)}, u32[]{:S(2)}, u32[]{:S(2)}) %collective-permute-start) | collective-permute-done | bytes 76832 | tf_op jit(solution)/shard_map/ppermute | solution.py:48
  7.5 2.0 %collective-permute-start.1 = (bf16[2,2,19200]{2,1,0:T(2,128)(2,1)S(1)}, bf16[2,2,19200]{2,1,0:T(2,128)(2,1)S(1)}, u32[]{:S(2)}, u32[]{:S(2)}) collective-permute-start(bf16[2,2,19200]{2,1,0:T(2,128)(2,1)S(1)} %bitcast_dynamic-update-slice_fusion.6), channel_id=1, source_target_pairs={{0,16},{2,6},{4,20},{6,10},{8,24},{10,14},{12,28},{14,2},{16,32},{... | collective-permute-start | bytes 460808 | tf_op jit(solution)/shard_map/ppermute | solution.py:48
  9.5 3.6 %collective-permute-start.2 = (bf16[2,2,19200]{2,1,0:T(2,128)(2,1)S(1)}, bf16[2,2,19200]{2,1,0:T(2,128)(2,1)S(1)}, u32[]{:S(2)}, u32[]{:S(2)}) collective-permute-start(bf16[2,2,19200]{2,1,0:T(2,128)(2,1)S(1)} %bitcast_dynamic-update-slice_fusion.6), channel_id=1, source_target_pairs={{0,32},{2,10},{4,36},{6,14},{8,40},{10,2},{12,44},{14,6},{16,48},{... | collective-permute-start | bytes 460808 | tf_op jit(solution)/shard_map/ppermute | solution.py:48
  13.1 1.0 collective-permute-start.3
  14.9 3.0 %collective-permute-done.2 = bf16[2,2,19200]{2,1,0:T(2,128)(2,1)S(1)} collective-permute-done((bf16[2,2,19200]{2,1,0:T(2,128)(2,1)S(1)}, bf16[2,2,19200]{2,1,0:T(2,128)(2,1)S(1)}, u32[]{:S(2)}, u32[]{:S(2)}) %collective-permute-start.2) | collective-permute-done | bytes 153632 | tf_op jit(solution)/shard_map/ppermute | solution.py:48
  18.7 1.6 %collective-permute-start.4 = (bf16[16,19200]{1,0:T(8,128)(2,1)S(1)}, bf16[16,19200]{1,0:T(8,128)(2,1)S(1)}, u32[]{:S(2)}, u32[]{:S(2)}) collective-permute-start(bf16[16,19200]{1,0:T(8,128)(2,1)S(1)} %reshape.26.refs_0_), channel_id=1, source_target_pairs={{0,4},{2,18},{4,8},{6,22},{8,12},{10,26},{12,0},{14,30},{16,20},{1... | collective-permute-start | bytes 1843208 | tf_op jit(solution)/shard_map/ppermute | solution.py:48
  20.3 2.9 %collective-permute-start.5 = (bf16[16,19200]{1,0:T(8,128)(2,1)S(1)}, bf16[16,19200]{1,0:T(8,128)(2,1)S(1)}, u32[]{:S(2)}, u32[]{:S(2)}) collective-permute-start(bf16[16,19200]{1,0:T(8,128)(2,1)S(1)} %reshape.26.refs_0_), channel_id=1, source_target_pairs={{0,8},{2,34},{4,12},{6,38},{8,0},{10,42},{12,4},{14,46},{16,24},{1... | collective-permute-start | bytes 1843208 | tf_op jit(solution)/shard_map/ppermute | solution.py:48
  23.2 1.3 collective-permute-start.6
  24.6 5.5 %collective-permute-done.4.refs_1_ = bf16[16,19200]{1,0:T(8,128)(2,1)S(1)} collective-permute-done((bf16[16,19200]{1,0:T(8,128)(2,1)S(1)}, bf16[16,19200]{1,0:T(8,128)(2,1)S(1)}, u32[]{:S(2)}, u32[]{:S(2)}) %collective-permute-start.4) | collective-permute-done | bytes 614432 | tf_op jit(solution)/shard_map/ppermute | solution.py:48
  30.1 7.8 %collective-permute-done.5.refs_2_ = bf16[16,19200]{1,0:T(8,128)(2,1)S(1)} collective-permute-done((bf16[16,19200]{1,0:T(8,128)(2,1)S(1)}, bf16[16,19200]{1,0:T(8,128)(2,1)S(1)}, u32[]{:S(2)}, u32[]{:S(2)}) %collective-permute-start.5) | collective-permute-done | bytes 614432 | tf_op jit(solution)/shard_map/ppermute | solution.py:48
  39.1 2.8 %collective-permute-done.7 = bf16[64,768]{1,0:T(8,128)(2,1)S(1)} collective-permute-done((bf16[64,768]{1,0:T(8,128)(2,1)S(1)}, bf16[64,768]{1,0:T(8,128)(2,1)S(1)}, u32[]{:S(2)}, u32[]{:S(2)}) %collective-permute-start.7) | collective-permute-done | bytes 98336 | tf_op jit(solution)/shard_map/ppermute | solution.py:48
  42.1 0.9 collective-permute-start.8
  43.0 3.1 %collective-permute-done.8 = bf16[144,128]{1,0:T(8,128)(2,1)S(1)} collective-permute-done((bf16[144,128]{1,0:T(8,128)(2,1)S(1)}, bf16[144,128]{1,0:T(8,128)(2,1)S(1)}, u32[]{:S(2)}, u32[]{:S(2)}) %collective-permute-start.8) | collective-permute-done | bytes 36896 | tf_op jit(solution)/shard_map/ppermute | solution.py:48
  48.7 1.1 collective-permute-start.13
  49.8 2.5 %collective-permute-start.14 = (bf16[288,128]{1,0:T(8,128)(2,1)S(1)}, bf16[288,128]{1,0:T(8,128)(2,1)S(1)}, u32[]{:S(2)}, u32[]{:S(2)}) collective-permute-start(bf16[288,128]{1,0:T(8,128)(2,1)S(1)} %pad_maximum_fusion), channel_id=1, source_target_pairs={{0,32},{2,10},{4,36},{6,14},{8,40},{10,2},{12,44},{14,6},{16,48},{... | collective-permute-start | bytes 221192 | tf_op jit(solution)/shard_map/ppermute | solution.py:48
  52.4 1.1 collective-permute-start.15
  54.3 1.4 collective-permute-done.14
  55.7 1.0 collective-permute-done.15
  58.6 1.6 %collective-permute-start.16 = (bf16[1152,128]{1,0:T(8,128)(2,1)}, bf16[1152,128]{1,0:T(8,128)(2,1)}, u32[]{:S(2)}, u32[]{:S(2)}) collective-permute-start(bf16[1152,128]{1,0:T(8,128)(2,1)} %constant_dynamic-update-slice_fusion.3.refs_0_), channel_id=1, source_target_pairs={{0,4},{2,18},{4,8},{6,22},{8,12},{10,26},{12,0},{14,30},{16,20},{1... | collective-permute-start | bytes 884744 | tf_op jit(solution)/shard_map/ppermute | solution.py:48
  60.3 2.1 %collective-permute-start.17 = (bf16[1152,128]{1,0:T(8,128)(2,1)}, bf16[1152,128]{1,0:T(8,128)(2,1)}, u32[]{:S(2)}, u32[]{:S(2)}) collective-permute-start(bf16[1152,128]{1,0:T(8,128)(2,1)} %constant_dynamic-update-slice_fusion.3.refs_0_), channel_id=1, source_target_pairs={{0,8},{2,34},{4,12},{6,38},{8,0},{10,42},{12,4},{14,46},{16,24},{1... | collective-permute-start | bytes 884744 | tf_op jit(solution)/shard_map/ppermute | solution.py:48
  62.4 1.7 %collective-permute-start.18 = (bf16[1152,128]{1,0:T(8,128)(2,1)}, bf16[1152,128]{1,0:T(8,128)(2,1)}, u32[]{:S(2)}, u32[]{:S(2)}) collective-permute-start(bf16[1152,128]{1,0:T(8,128)(2,1)} %constant_dynamic-update-slice_fusion.3.refs_0_), channel_id=1, source_target_pairs={{0,12},{2,50},{4,0},{6,54},{8,4},{10,58},{12,8},{14,62},{16,28},{1... | collective-permute-start | bytes 884744 | tf_op jit(solution)/shard_map/ppermute | solution.py:48
  64.1 2.8 %collective-permute-done.16.refs_1_ = bf16[1152,128]{1,0:T(8,128)(2,1)} collective-permute-done((bf16[1152,128]{1,0:T(8,128)(2,1)}, bf16[1152,128]{1,0:T(8,128)(2,1)}, u32[]{:S(2)}, u32[]{:S(2)}) %collective-permute-start.16) | collective-permute-done | bytes 294944 | tf_op jit(solution)/shard_map/ppermute | solution.py:48
  66.9 3.7 %collective-permute-done.17.refs_2_ = bf16[1152,128]{1,0:T(8,128)(2,1)} collective-permute-done((bf16[1152,128]{1,0:T(8,128)(2,1)}, bf16[1152,128]{1,0:T(8,128)(2,1)}, u32[]{:S(2)}, u32[]{:S(2)}) %collective-permute-start.17) | collective-permute-done | bytes 294944 | tf_op jit(solution)/shard_map/ppermute | solution.py:48
  71.5 1.1 copy-done.2
  72.6 1.1 copy-done.4
  73.7 1.1 copy-done.6
  74.8 4.3 %shard_map.138 = (bf16[128,9216]{1,0:T(8,128)(2,1)S(1)}, bf16[128,9216]{1,0:T(8,128)(2,1)S(1)}, f32[144,128]{1,0:T(8,128)S(1)}, bf16[16,9216]{1,0:T(8,128)(2,1)S(1)}) custom-call(s32[5]{0:T(128)S(1)} %stack.23.place, bf16[16,19200]{1,0:T(8,128)(2,1)S(1)} %reshape.26.refs_0_, bf16[16,19200]{1,0:T(8,128)(2,1)S(1)} %collective-permute-done.4.refs_1_, ...), custom_call_target="tpu_custom_call" | custom-call | bytes 18450000 | tf_op jit(solution)/shard_map/pallas_call | solution.py:328
  79.1 20.5 %shard_map.139 = (bf16[3584,128]{1,0:T(8,128)(2,1)S(1)}, bf16[3584,128]{1,0:T(8,128)(2,1)S(1)}, bf16[3584,128]{1,0:T(8,128)(2,1)S(1)}, bf16[3584,128]{1,0:T(8,12...) custom-call(s32[5]{0:T(128)S(1)} %stack.23.place, ...), custom_call_target="tpu_custom_call" | custom-call | bytes 73800000 | tf_op jit(solution)/shard_map/pallas_call | solution.py:328
  100.8 1.5 collective-permute-done.27
  102.5 2.1 %collective-permute-start.28 = (bf16[3584,128]{1,0:T(8,128)(2,1)S(1)}, bf16[3584,128]{1,0:T(8,128)(2,1)S(1)}, u32[]{:S(2)}, u32[]{:S(2)}) collective-permute-start(bf16[3584,128]{1,0:T(8,128)(2,1)S(1)} %add_convert_fusion), channel_id=1, source_target_pairs={{0,4},{2,18},{4,8},{6,22},{8,12},{10,26},{12,0},{14,30},{16,20},{1... | collective-permute-start | bytes 2752520 | tf_op jit(solution)/shard_map/ppermute | solution.py:48
  104.9 1.7 %collective-permute-start.26 = (bf16[3584,128]{1,0:T(8,128)(2,1)S(1)}, bf16[3584,128]{1,0:T(8,128)(2,1)S(1)}, u32[]{:S(2)}, u32[]{:S(2)}) collective-permute-start(bf16[3584,128]{1,0:T(8,128)(2,1)S(1)} %add_convert_fusion.1), channel_id=1, source_target_pairs={{0,12},{2,50},{4,0},{6,54},{8,4},{10,58},{12,8},{14,62},{16,28},{1... | collective-permute-start | bytes 2752520 | tf_op jit(solution)/shard_map/ppermute | solution.py:48
  106.8 1.5 collective-permute-start.24
  108.3 1.4 collective-permute-start.30
  109.7 5.8 %collective-permute-done.30.refs_5_ = bf16[128,768]{1,0:T(8,128)(2,1)S(1)} collective-permute-done((bf16[128,768]{1,0:T(8,128)(2,1)S(1)}, bf16[128,768]{1,0:T(8,128)(2,1)S(1)}, u32[]{:S(2)}, u32[]{:S(2)}) %collective-permute-start.30) | collective-permute-done | bytes 196640 | tf_op jit(solution)/shard_map/ppermute | solution.py:386
  115.5 1.7 %collective-permute-done.28.refs_3_ = bf16[3584,128]{1,0:T(8,128)(2,1)S(1)} collective-permute-done((bf16[3584,128]{1,0:T(8,128)(2,1)S(1)}, bf16[3584,128]{1,0:T(8,128)(2,1)S(1)}, u32[]{:S(2)}, u32[]{:S(2)}) %collective-permute-start.28) | collective-permute-done | bytes 917536 | tf_op jit(solution)/shard_map/ppermute | solution.py:48
  117.2 1.1 collective-permute-done.26.refs_2_
  118.3 9.6 %collective-permute-done.24.refs_1_ = bf16[3584,128]{1,0:T(8,128)(2,1)S(1)} collective-permute-done((bf16[3584,128]{1,0:T(8,128)(2,1)S(1)}, bf16[3584,128]{1,0:T(8,128)(2,1)S(1)}, u32[]{:S(2)}, u32[]{:S(2)}) %collective-permute-start.24) | collective-permute-done | bytes 917536 | tf_op jit(solution)/shard_map/ppermute | solution.py:48
  127.9 2.1 %shard_map.140 = (f32[2,448,128]{2,1,0:T(8,128)S(1)}, bf16[2,448,128]{2,1,0:T(8,128)(2,1)S(1)}, bf16[2,448,128]{2,1,0:T(8,128)(2,1)S(1)}, bf16[2,448,128]{2,1,0:T(8,128)(2,1)S(1)}) custom-call(s32[5]{0:T(128)S(1)} %stack.23.place, bf16[3584,128]{1,0:T(8,128)(2,1)S(1)} %get-tuple-element.63.refs_0_, bf16[3584,128]{1,0:T(8,128)(2,1)S(1)} %collective-permute-done.24.refs_1_, ...), custom_call_target="tpu_custom_call" | custom-call | bytes 11070000 | tf_op jit(solution)/shard_map/pallas_call | solution.py:328
  130.0 2.4 %collective-permute-start.31 = (bf16[2,448,128]{2,1,0:T(8,128)(2,1)S(1)}, bf16[2,448,128]{2,1,0:T(8,128)(2,1)S(1)}, u32[]{:S(2)}, u32[]{:S(2)}) collective-permute-start(bf16[2,448,128]{2,1,0:T(8,128)(2,1)S(1)} %get-tuple-element.72), channel_id=1, source_target_pairs={{0,48},{2,14},{4,52},{6,2},{8,56},{10,6},{12,60},{14,10},{16,0},{1... | collective-permute-start | bytes 688136 | tf_op jit(solution)/shard_map/ppermute | solution.py:48
  133.5 5.0 %collective-permute-done.31 = bf16[2,448,128]{2,1,0:T(8,128)(2,1)S(1)} collective-permute-done((bf16[2,448,128]{2,1,0:T(8,128)(2,1)S(1)}, bf16[2,448,128]{2,1,0:T(8,128)(2,1)S(1)}, u32[]{:S(2)}, u32[]{:S(2)}) %collective-permute-start.31) | collective-permute-done | bytes 229408 | tf_op jit(solution)/shard_map/ppermute | solution.py:48
  138.5 1.6 %collective-permute-done.32 = bf16[2,448,128]{2,1,0:T(8,128)(2,1)S(1)} collective-permute-done((bf16[2,448,128]{2,1,0:T(8,128)(2,1)S(1)}, bf16[2,448,128]{2,1,0:T(8,128)(2,1)S(1)}, u32[]{:S(2)}, u32[]{:S(2)}) %collective-permute-start.32) | collective-permute-done | bytes 229408 | tf_op jit(solution)/shard_map/ppermute | solution.py:48
  140.1 2.4 %collective-permute-done.33 = bf16[2,448,128]{2,1,0:T(8,128)(2,1)S(1)} collective-permute-done((bf16[2,448,128]{2,1,0:T(8,128)(2,1)S(1)}, bf16[2,448,128]{2,1,0:T(8,128)(2,1)S(1)}, u32[]{:S(2)}, u32[]{:S(2)}) %collective-permute-start.33) | collective-permute-done | bytes 229408 | tf_op jit(solution)/shard_map/ppermute | solution.py:48
  142.5 0.9 collective-permute-start.34
  143.4 4.4 %collective-permute-done.34 = bf16[448,128]{1,0:T(8,128)(2,1)S(1)} collective-permute-done((bf16[448,128]{1,0:T(8,128)(2,1)S(1)}, bf16[448,128]{1,0:T(8,128)(2,1)S(1)}, u32[]{:S(2)}, u32[]{:S(2)}) %collective-permute-start.34) | collective-permute-done | bytes 114720 | tf_op jit(solution)/shard_map/ppermute | solution.py:48
  148.1 1.1 collective-permute-start.35
  150.4 3.2 %collective-permute-done.35 = bf16[144,128]{1,0:T(8,128)(2,1)S(1)} collective-permute-done((bf16[144,128]{1,0:T(8,128)(2,1)S(1)}, bf16[144,128]{1,0:T(8,128)(2,1)S(1)}, u32[]{:S(2)}, u32[]{:S(2)}) %collective-permute-start.35) | collective-permute-done | bytes 36896 | tf_op jit(solution)/shard_map/ppermute | solution.py:471
  153.8 1.0 convolution_add_fusion
  (102 shorter events, 17.2 us)
Async XLA Ops:
  0.6 41.2 %copy-start = (bf16[768,144]{0,1:T(8,128)(2,1)S(1)}, bf16[768,144]{0,1:T(8,128)(2,1)}, u32[]{:S(2)}) copy-start(bf16[768,144]{0,1:T(8,128)(2,1)} %param.12) | copy-start | bytes 663556
  3.0 4.5 %collective-permute-start = (bf16[2,19200]{1,0:T(2,128)(2,1)S(1)}, bf16[2,19200]{1,0:T(2,128)(2,1)S(1)}, u32[]{:S(2)}, u32[]{:S(2)}) collective-permute-start(bf16[2,19200]{1,0:T(2,128)(2,1)S(1)} %constant_dynamic-update-slice_fusion), channel_id=1, source_target_pairs={{0,64},{2,66},{4,68},{6,70},{8,72},{10,74},{12,76},{14,78},{16,80}... | collective-permute-start | bytes 230408 | tf_op jit(solution)/shard_map/ppermute | solution.py:48
  4.0 20.6 %copy-start.13 = (bf16[144]{0:T(256)(128)(2,1)S(1)}, bf16[144]{0:T(256)(128)(2,1)}, u32[]{:S(2)}) copy-start(bf16[144]{0:T(256)(128)(2,1)} %param.13) | copy-start | bytes 868
  7.5 7.3 %collective-permute-start.1 = (bf16[2,2,19200]{2,1,0:T(2,128)(2,1)S(1)}, bf16[2,2,19200]{2,1,0:T(2,128)(2,1)S(1)}, u32[]{:S(2)}, u32[]{:S(2)}) collective-permute-start(bf16[2,2,19200]{2,1,0:T(2,128)(2,1)S(1)} %bitcast_dynamic-update-slice_fusion.6), channel_id=1, source_target_pairs={{0,16},{2,6},{4,20},{6,10},{8,24},{10,14},{12,28},{14,2},{16,32},{... | collective-permute-start | bytes 460808 | tf_op jit(solution)/shard_map/ppermute | solution.py:48
  9.5 8.4 %collective-permute-start.2 = (bf16[2,2,19200]{2,1,0:T(2,128)(2,1)S(1)}, bf16[2,2,19200]{2,1,0:T(2,128)(2,1)S(1)}, u32[]{:S(2)}, u32[]{:S(2)}) collective-permute-start(bf16[2,2,19200]{2,1,0:T(2,128)(2,1)S(1)} %bitcast_dynamic-update-slice_fusion.6), channel_id=1, source_target_pairs={{0,32},{2,10},{4,36},{6,14},{8,40},{10,2},{12,44},{14,6},{16,48},{... | collective-permute-start | bytes 460808 | tf_op jit(solution)/shard_map/ppermute | solution.py:48
  13.1 5.2 %collective-permute-start.3 = (bf16[2,2,19200]{2,1,0:T(2,128)(2,1)S(1)}, bf16[2,2,19200]{2,1,0:T(2,128)(2,1)S(1)}, u32[]{:S(2)}, u32[]{:S(2)}) collective-permute-start(bf16[2,2,19200]{2,1,0:T(2,128)(2,1)S(1)} %bitcast_dynamic-update-slice_fusion.6), channel_id=1, source_target_pairs={{0,48},{2,14},{4,52},{6,2},{8,56},{10,6},{12,60},{14,10},{16,0},{1... | collective-permute-start | bytes 460808 | tf_op jit(solution)/shard_map/ppermute | solution.py:48
  18.0 53.4 %copy-start.12 = (bf16[576]{0:T(1024)(128)(2,1)S(1)}, bf16[576]{0:T(1024)(128)(2,1)}, u32[]{:S(2)}) copy-start(bf16[576]{0:T(1024)(128)(2,1)} %param.18) | copy-start | bytes 3460
  18.1 53.5 %copy-start.7 = (f32[9216]{0:T(1024)S(1)}, f32[9216]{0:T(1024)}, u32[]{:S(2)}) copy-start(f32[9216]{0:T(1024)} %param.15) | copy-start | bytes 110596
  18.1 53.5 %copy-start.8 = (f32[9216]{0:T(1024)S(1)}, f32[9216]{0:T(1024)}, u32[]{:S(2)}) copy-start(f32[9216]{0:T(1024)} %param.16) | copy-start | bytes 110596
  18.7 11.4 %collective-permute-start.4 = (bf16[16,19200]{1,0:T(8,128)(2,1)S(1)}, bf16[16,19200]{1,0:T(8,128)(2,1)S(1)}, u32[]{:S(2)}, u32[]{:S(2)}) collective-permute-start(bf16[16,19200]{1,0:T(8,128)(2,1)S(1)} %reshape.26.refs_0_), channel_id=1, source_target_pairs={{0,4},{2,18},{4,8},{6,22},{8,12},{10,26},{12,0},{14,30},{16,20},{1... | collective-permute-start | bytes 1843208 | tf_op jit(solution)/shard_map/ppermute | solution.py:48
  20.3 17.6 %collective-permute-start.5 = (bf16[16,19200]{1,0:T(8,128)(2,1)S(1)}, bf16[16,19200]{1,0:T(8,128)(2,1)S(1)}, u32[]{:S(2)}, u32[]{:S(2)}) collective-permute-start(bf16[16,19200]{1,0:T(8,128)(2,1)S(1)} %reshape.26.refs_0_), channel_id=1, source_target_pairs={{0,8},{2,34},{4,12},{6,38},{8,0},{10,42},{12,4},{14,46},{16,24},{1... | collective-permute-start | bytes 1843208 | tf_op jit(solution)/shard_map/ppermute | solution.py:48
  23.2 14.7 %collective-permute-start.6 = (bf16[16,19200]{1,0:T(8,128)(2,1)S(1)}, bf16[16,19200]{1,0:T(8,128)(2,1)S(1)}, u32[]{:S(2)}, u32[]{:S(2)}) collective-permute-start(bf16[16,19200]{1,0:T(8,128)(2,1)S(1)} %reshape.26.refs_0_), channel_id=1, source_target_pairs={{0,12},{2,50},{4,0},{6,54},{8,4},{10,58},{12,8},{14,62},{16,28},{1... | collective-permute-start | bytes 1843208 | tf_op jit(solution)/shard_map/ppermute | solution.py:48
  24.6 21.6 %collective-permute-start.9 = (bf16[16,19200]{1,0:T(8,128)(2,1)S(1)}, bf16[16,19200]{1,0:T(8,128)(2,1)S(1)}, u32[]{:S(2)}, u32[]{:S(2)}) collective-permute-start(bf16[16,19200]{1,0:T(8,128)(2,1)S(1)} %reshape.26.refs_0_), channel_id=1, source_target_pairs={{0,2},{2,0},{4,6},{6,4},{8,10},{10,8},{12,14},{14,12},{16,18},{18,... | collective-permute-start | bytes 1843208 | tf_op jit(solution)/shard_map/ppermute | solution.py:48
  37.9 8.3 %collective-permute-start.10 = (bf16[16,19200]{1,0:T(8,128)(2,1)S(1)}, bf16[16,19200]{1,0:T(8,128)(2,1)S(1)}, u32[]{:S(2)}, u32[]{:S(2)}) collective-permute-start(bf16[16,19200]{1,0:T(8,128)(2,1)S(1)} %collective-permute-done.4.refs_1_), channel_id=1, source_target_pairs={{0,2},{2,0},{4,6},{6,4},{8,10},{10,8},{12,14},{14,12},{16,18},{18,... | collective-permute-start | bytes 1843208 | tf_op jit(solution)/shard_map/ppermute | solution.py:48
  37.9 9.1 %collective-permute-start.11 = (bf16[16,19200]{1,0:T(8,128)(2,1)S(1)}, bf16[16,19200]{1,0:T(8,128)(2,1)S(1)}, u32[]{:S(2)}, u32[]{:S(2)}) collective-permute-start(bf16[16,19200]{1,0:T(8,128)(2,1)S(1)} %collective-permute-done.5.refs_2_), channel_id=1, source_target_pairs={{0,2},{2,0},{4,6},{6,4},{8,10},{10,8},{12,14},{14,12},{16,18},{18,... | collective-permute-start | bytes 1843208 | tf_op jit(solution)/shard_map/ppermute | solution.py:48
  38.4 9.5 %collective-permute-start.12 = (bf16[16,19200]{1,0:T(8,128)(2,1)S(1)}, bf16[16,19200]{1,0:T(8,128)(2,1)S(1)}, u32[]{:S(2)}, u32[]{:S(2)}) collective-permute-start(bf16[16,19200]{1,0:T(8,128)(2,1)S(1)} %collective-permute-done.6.refs_3_), channel_id=1, source_target_pairs={{0,2},{2,0},{4,6},{6,4},{8,10},{10,8},{12,14},{14,12},{16,18},{18,... | collective-permute-start | bytes 1843208 | tf_op jit(solution)/shard_map/ppermute | solution.py:48
  38.5 3.4 %collective-permute-start.7 = (bf16[64,768]{1,0:T(8,128)(2,1)S(1)}, bf16[64,768]{1,0:T(8,128)(2,1)S(1)}, u32[]{:S(2)}, u32[]{:S(2)}) collective-permute-start(bf16[64,768]{1,0:T(8,128)(2,1)S(1)} %bitcast.69), channel_id=1, source_target_pairs={{0,2},{2,0},{4,6},{6,4},{8,10},{10,8},{12,14},{14,12},{16,18},{18,... | collective-permute-start | bytes 294920 | tf_op jit(solution)/shard_map/ppermute | solution.py:48
  41.9 29.6 %copy-start.10 = (bf16[2,64,768]{2,1,0:T(8,128)(2,1)}, bf16[2,64,768]{2,1,0:T(8,128)(2,1)S(1)}, u32[]{:S(2)}) copy-start(bf16[2,64,768]{2,1,0:T(8,128)(2,1)S(1)} %bitcast_dynamic-update-slice_fusion.4) | copy-start | bytes 589828
  42.1 4.0 %collective-permute-start.8 = (bf16[144,128]{1,0:T(8,128)(2,1)S(1)}, bf16[144,128]{1,0:T(8,128)(2,1)S(1)}, u32[]{:S(2)}, u32[]{:S(2)}) collective-permute-start(bf16[144,128]{1,0:T(8,128)(2,1)S(1)} %fusion.1), channel_id=1, source_target_pairs={{0,64},{2,66},{4,68},{6,70},{8,72},{10,74},{12,76},{14,78},{16,80}... | collective-permute-start | bytes 110600 | tf_op jit(solution)/shard_map/ppermute | solution.py:48
  47.0 0.9 copy-start.3
  48.7 5.6 %collective-permute-start.13 = (bf16[288,128]{1,0:T(8,128)(2,1)S(1)}, bf16[288,128]{1,0:T(8,128)(2,1)S(1)}, u32[]{:S(2)}, u32[]{:S(2)}) collective-permute-start(bf16[288,128]{1,0:T(8,128)(2,1)S(1)} %pad_maximum_fusion), channel_id=1, source_target_pairs={{0,16},{2,6},{4,20},{6,10},{8,24},{10,14},{12,28},{14,2},{16,32},{... | collective-permute-start | bytes 221192 | tf_op jit(solution)/shard_map/ppermute | solution.py:48
  49.8 5.9 %collective-permute-start.14 = (bf16[288,128]{1,0:T(8,128)(2,1)S(1)}, bf16[288,128]{1,0:T(8,128)(2,1)S(1)}, u32[]{:S(2)}, u32[]{:S(2)}) collective-permute-start(bf16[288,128]{1,0:T(8,128)(2,1)S(1)} %pad_maximum_fusion), channel_id=1, source_target_pairs={{0,32},{2,10},{4,36},{6,14},{8,40},{10,2},{12,44},{14,6},{16,48},{... | collective-permute-start | bytes 221192 | tf_op jit(solution)/shard_map/ppermute | solution.py:48
  52.4 4.4 %collective-permute-start.15 = (bf16[288,128]{1,0:T(8,128)(2,1)S(1)}, bf16[288,128]{1,0:T(8,128)(2,1)S(1)}, u32[]{:S(2)}, u32[]{:S(2)}) collective-permute-start(bf16[288,128]{1,0:T(8,128)(2,1)S(1)} %pad_maximum_fusion), channel_id=1, source_target_pairs={{0,48},{2,14},{4,52},{6,2},{8,56},{10,6},{12,60},{14,10},{16,0},{1... | collective-permute-start | bytes 221192 | tf_op jit(solution)/shard_map/ppermute | solution.py:48
  58.6 8.2 %collective-permute-start.16 = (bf16[1152,128]{1,0:T(8,128)(2,1)}, bf16[1152,128]{1,0:T(8,128)(2,1)}, u32[]{:S(2)}, u32[]{:S(2)}) collective-permute-start(bf16[1152,128]{1,0:T(8,128)(2,1)} %constant_dynamic-update-slice_fusion.3.refs_0_), channel_id=1, source_target_pairs={{0,4},{2,18},{4,8},{6,22},{8,12},{10,26},{12,0},{14,30},{16,20},{1... | collective-permute-start | bytes 884744 | tf_op jit(solution)/shard_map/ppermute | solution.py:48
  60.3 10.3 %collective-permute-start.17 = (bf16[1152,128]{1,0:T(8,128)(2,1)}, bf16[1152,128]{1,0:T(8,128)(2,1)}, u32[]{:S(2)}, u32[]{:S(2)}) collective-permute-start(bf16[1152,128]{1,0:T(8,128)(2,1)} %constant_dynamic-update-slice_fusion.3.refs_0_), channel_id=1, source_target_pairs={{0,8},{2,34},{4,12},{6,38},{8,0},{10,42},{12,4},{14,46},{16,24},{1... | collective-permute-start | bytes 884744 | tf_op jit(solution)/shard_map/ppermute | solution.py:48
  62.4 8.5 %collective-permute-start.18 = (bf16[1152,128]{1,0:T(8,128)(2,1)}, bf16[1152,128]{1,0:T(8,128)(2,1)}, u32[]{:S(2)}, u32[]{:S(2)}) collective-permute-start(bf16[1152,128]{1,0:T(8,128)(2,1)} %constant_dynamic-update-slice_fusion.3.refs_0_), channel_id=1, source_target_pairs={{0,12},{2,50},{4,0},{6,54},{8,4},{10,58},{12,8},{14,62},{16,28},{1... | collective-permute-start | bytes 884744 | tf_op jit(solution)/shard_map/ppermute | solution.py:48
  64.1 14.9 %collective-permute-start.19 = (bf16[1152,128]{1,0:T(8,128)(2,1)}, bf16[1152,128]{1,0:T(8,128)(2,1)}, u32[]{:S(2)}, u32[]{:S(2)}) collective-permute-start(bf16[1152,128]{1,0:T(8,128)(2,1)} %constant_dynamic-update-slice_fusion.3.refs_0_), channel_id=1, source_target_pairs={{0,2},{2,0},{4,6},{6,4},{8,10},{10,8},{12,14},{14,12},{16,18},{18,... | collective-permute-start | bytes 884744 | tf_op jit(solution)/shard_map/ppermute | solution.py:48
  70.9 8.2 %collective-permute-start.20 = (bf16[1152,128]{1,0:T(8,128)(2,1)}, bf16[1152,128]{1,0:T(8,128)(2,1)}, u32[]{:S(2)}, u32[]{:S(2)}) collective-permute-start(bf16[1152,128]{1,0:T(8,128)(2,1)} %collective-permute-done.16.refs_1_), channel_id=1, source_target_pairs={{0,2},{2,0},{4,6},{6,4},{8,10},{10,8},{12,14},{14,12},{16,18},{18,... | collective-permute-start | bytes 884744 | tf_op jit(solution)/shard_map/ppermute | solution.py:48
  70.9 8.2 %collective-permute-start.21 = (bf16[1152,128]{1,0:T(8,128)(2,1)}, bf16[1152,128]{1,0:T(8,128)(2,1)}, u32[]{:S(2)}, u32[]{:S(2)}) collective-permute-start(bf16[1152,128]{1,0:T(8,128)(2,1)} %collective-permute-done.17.refs_2_), channel_id=1, source_target_pairs={{0,2},{2,0},{4,6},{6,4},{8,10},{10,8},{12,14},{14,12},{16,18},{18,... | collective-permute-start | bytes 884744 | tf_op jit(solution)/shard_map/ppermute | solution.py:48
  71.4 7.7 %collective-permute-start.22 = (bf16[1152,128]{1,0:T(8,128)(2,1)}, bf16[1152,128]{1,0:T(8,128)(2,1)}, u32[]{:S(2)}, u32[]{:S(2)}) collective-permute-start(bf16[1152,128]{1,0:T(8,128)(2,1)} %collective-permute-done.18.refs_3_), channel_id=1, source_target_pairs={{0,2},{2,0},{4,6},{6,4},{8,10},{10,8},{12,14},{14,12},{16,18},{18,... | collective-permute-start | bytes 884744 | tf_op jit(solution)/shard_map/ppermute | solution.py:48
  71.5 1.1 copy-start.2
  72.6 1.1 copy-start.4
  73.7 1.1 copy-start.6
  74.8 4.3 %copy-start.9 = (f32[9216]{0:T(1024)S(1)}, f32[9216]{0:T(1024)}, u32[]{:S(2)}) copy-start(f32[9216]{0:T(1024)} %param.20) | copy-start | bytes 110596
  99.6 2.7 %collective-permute-start.27 = (bf16[3584,128]{1,0:T(8,128)(2,1)S(1)}, bf16[3584,128]{1,0:T(8,128)(2,1)S(1)}, u32[]{:S(2)}, u32[]{:S(2)}) collective-permute-start(bf16[3584,128]{1,0:T(8,128)(2,1)S(1)} %get-tuple-element.69), channel_id=1, source_target_pairs={{0,2},{2,0},{4,6},{6,4},{8,10},{10,8},{12,14},{14,12},{16,18},{18,... | collective-permute-start | bytes 2752520 | tf_op jit(solution)/shard_map/ppermute | solution.py:48
  100.2 4.4 %collective-permute-start.25 = (bf16[3584,128]{1,0:T(8,128)(2,1)S(1)}, bf16[3584,128]{1,0:T(8,128)(2,1)S(1)}, u32[]{:S(2)}, u32[]{:S(2)}) collective-permute-start(bf16[3584,128]{1,0:T(8,128)(2,1)S(1)} %get-tuple-element.67), channel_id=1, source_target_pairs={{0,2},{2,0},{4,6},{6,4},{8,10},{10,8},{12,14},{14,12},{16,18},{18,... | collective-permute-start | bytes 2752520 | tf_op jit(solution)/shard_map/ppermute | solution.py:48
  100.3 6.3 %collective-permute-start.23 = (bf16[3584,128]{1,0:T(8,128)(2,1)S(1)}, bf16[3584,128]{1,0:T(8,128)(2,1)S(1)}, u32[]{:S(2)}, u32[]{:S(2)}) collective-permute-start(bf16[3584,128]{1,0:T(8,128)(2,1)S(1)} %get-tuple-element.65), channel_id=1, source_target_pairs={{0,2},{2,0},{4,6},{6,4},{8,10},{10,8},{12,14},{14,12},{16,18},{18,... | collective-permute-start | bytes 2752520 | tf_op jit(solution)/shard_map/ppermute | solution.py:48
  100.7 14.8 %collective-permute-start.29 = (bf16[3584,128]{1,0:T(8,128)(2,1)S(1)}, bf16[3584,128]{1,0:T(8,128)(2,1)S(1)}, u32[]{:S(2)}, u32[]{:S(2)}) collective-permute-start(bf16[3584,128]{1,0:T(8,128)(2,1)S(1)} %get-tuple-element.70), channel_id=1, source_target_pairs={{0,2},{2,0},{4,6},{6,4},{8,10},{10,8},{12,14},{14,12},{16,18},{18,... | collective-permute-start | bytes 2752520 | tf_op jit(solution)/shard_map/ppermute | solution.py:48
  102.5 14.7 %collective-permute-start.28 = (bf16[3584,128]{1,0:T(8,128)(2,1)S(1)}, bf16[3584,128]{1,0:T(8,128)(2,1)S(1)}, u32[]{:S(2)}, u32[]{:S(2)}) collective-permute-start(bf16[3584,128]{1,0:T(8,128)(2,1)S(1)} %add_convert_fusion), channel_id=1, source_target_pairs={{0,4},{2,18},{4,8},{6,22},{8,12},{10,26},{12,0},{14,30},{16,20},{1... | collective-permute-start | bytes 2752520 | tf_op jit(solution)/shard_map/ppermute | solution.py:48
  104.8 3.5 %copy-start.11 = (bf16[2,64,768]{2,1,0:T(8,128)(2,1)S(1)}, bf16[2,64,768]{2,1,0:T(8,128)(2,1)}, u32[]{:S(2)}) copy-start(bf16[2,64,768]{2,1,0:T(8,128)(2,1)} %copy-done.10) | copy-start | bytes 589828
  104.9 13.5 %collective-permute-start.26 = (bf16[3584,128]{1,0:T(8,128)(2,1)S(1)}, bf16[3584,128]{1,0:T(8,128)(2,1)S(1)}, u32[]{:S(2)}, u32[]{:S(2)}) collective-permute-start(bf16[3584,128]{1,0:T(8,128)(2,1)S(1)} %add_convert_fusion.1), channel_id=1, source_target_pairs={{0,12},{2,50},{4,0},{6,54},{8,4},{10,58},{12,8},{14,62},{16,28},{1... | collective-permute-start | bytes 2752520 | tf_op jit(solution)/shard_map/ppermute | solution.py:48
  106.8 21.1 %collective-permute-start.24 = (bf16[3584,128]{1,0:T(8,128)(2,1)S(1)}, bf16[3584,128]{1,0:T(8,128)(2,1)S(1)}, u32[]{:S(2)}, u32[]{:S(2)}) collective-permute-start(bf16[3584,128]{1,0:T(8,128)(2,1)S(1)} %add_convert_fusion.2), channel_id=1, source_target_pairs={{0,8},{2,34},{4,12},{6,38},{8,0},{10,42},{12,4},{14,46},{16,24},{1... | collective-permute-start | bytes 2752520 | tf_op jit(solution)/shard_map/ppermute | solution.py:48
  108.3 7.2 %collective-permute-start.30 = (bf16[128,768]{1,0:T(8,128)(2,1)S(1)}, bf16[128,768]{1,0:T(8,128)(2,1)S(1)}, u32[]{:S(2)}, u32[]{:S(2)}) collective-permute-start(bf16[128,768]{1,0:T(8,128)(2,1)S(1)} %bitcast.67), channel_id=1, source_target_pairs={{0,1},{1,0},{2,3},{3,2},{4,5},{5,4},{6,7},{7,6},{8,9},{9,8},{10,11... | collective-permute-start | bytes 589832 | tf_op jit(solution)/shard_map/ppermute | solution.py:386
  130.0 8.4 %collective-permute-start.31 = (bf16[2,448,128]{2,1,0:T(8,128)(2,1)S(1)}, bf16[2,448,128]{2,1,0:T(8,128)(2,1)S(1)}, u32[]{:S(2)}, u32[]{:S(2)}) collective-permute-start(bf16[2,448,128]{2,1,0:T(8,128)(2,1)S(1)} %get-tuple-element.72), channel_id=1, source_target_pairs={{0,48},{2,14},{4,52},{6,2},{8,56},{10,6},{12,60},{14,10},{16,0},{1... | collective-permute-start | bytes 688136 | tf_op jit(solution)/shard_map/ppermute | solution.py:48
  132.4 7.6 %collective-permute-start.32 = (bf16[2,448,128]{2,1,0:T(8,128)(2,1)S(1)}, bf16[2,448,128]{2,1,0:T(8,128)(2,1)S(1)}, u32[]{:S(2)}, u32[]{:S(2)}) collective-permute-start(bf16[2,448,128]{2,1,0:T(8,128)(2,1)S(1)} %get-tuple-element.73), channel_id=1, source_target_pairs={{0,32},{2,10},{4,36},{6,14},{8,40},{10,2},{12,44},{14,6},{16,48},{... | collective-permute-start | bytes 688136 | tf_op jit(solution)/shard_map/ppermute | solution.py:48
  132.9 9.5 %collective-permute-start.33 = (bf16[2,448,128]{2,1,0:T(8,128)(2,1)S(1)}, bf16[2,448,128]{2,1,0:T(8,128)(2,1)S(1)}, u32[]{:S(2)}, u32[]{:S(2)}) collective-permute-start(bf16[2,448,128]{2,1,0:T(8,128)(2,1)S(1)} %get-tuple-element.74), channel_id=1, source_target_pairs={{0,16},{2,6},{4,20},{6,10},{8,24},{10,14},{12,28},{14,2},{16,32},{... | collective-permute-start | bytes 688136 | tf_op jit(solution)/shard_map/ppermute | solution.py:48
  142.5 5.3 %collective-permute-start.34 = (bf16[448,128]{1,0:T(8,128)(2,1)S(1)}, bf16[448,128]{1,0:T(8,128)(2,1)S(1)}, u32[]{:S(2)}, u32[]{:S(2)}) collective-permute-start(bf16[448,128]{1,0:T(8,128)(2,1)S(1)} %fusion.3), channel_id=1, source_target_pairs={{0,64},{2,66},{4,68},{6,70},{8,72},{10,74},{12,76},{14,78},{16,80}... | collective-permute-start | bytes 344072 | tf_op jit(solution)/shard_map/ppermute | solution.py:48
  148.1 5.5 %collective-permute-start.35 = (bf16[144,128]{1,0:T(8,128)(2,1)S(1)}, bf16[144,128]{1,0:T(8,128)(2,1)S(1)}, u32[]{:S(2)}, u32[]{:S(2)}) collective-permute-start(bf16[144,128]{1,0:T(8,128)(2,1)S(1)} %get-tuple-element.81), channel_id=1, source_target_pairs={{0,1},{1,0},{2,3},{3,2},{4,5},{5,4},{6,7},{7,6},{8,9},{9,8},{10,11... | collective-permute-start | bytes 110600 | tf_op jit(solution)/shard_map/ppermute | solution.py:471
  (2 other events, 1.6 us)

commit v2 on v1

--- a/solution.py
+++ b/solution.py
@@ -368,7 +368,8 @@
     nw = rows * width // LANES
 
     def around(value, stage):
-        return [value, *lax.optimization_barrier([send(value, ring_pairs(stage, k)) for k in (1, 2, 3)])]
+        two, one, three = lax.optimization_barrier([send(value, ring_pairs(stage, k)) for k in (2, 1, 3)])
+        return [value, one, two, three]
 
     pack = jnp.concatenate([queries, captions, cotangent], axis=1)
     pack = gather2(pack, "x", x)
@@ -439,7 +440,7 @@
     )
 
     got = []
-    for k in (2, 1, 3, 0):
+    for k in (1, 3, 2, 0):
         part = send(parts[4 + k], swap_pairs("core"))
         if k:
             part = (parts[k].astype(F32) + part.astype(F32)).astype(BF16)

time: 156 us -> 154 us (0.987)
  waiting for transfers between devices: 71.5 us -> 67.7 us
  starting transfers between devices: 39.4 us -> 41.6 us
    ppermute x34, waiting for transfers between devices: 62.6 us -> 57.8 us  [send(): return lax.ppermute(value, 'fsdp', pairs)]
    ppermute x34, starting transfers between devices: 36.9 us -> 39 us  [send(): return lax.ppermute(value, 'fsdp', pairs)]
  transfers between devices with their start and end apart: 36 -> 36, of which waited for: 24 -> 21; matrix products, arithmetic and copies ran while one was open for 3% -> 3% of each run, Pallas kernels for 3% -> 3%
where the time goes in v2:
time: 154 us
  waiting for transfers between devices  67.7 us (44%)
  starting transfers between devices  41.6 us (27%)
  Pallas kernels  26.9 us (17%)
  local copies, waits for them, and re-layouts  13.5 us (9%)
  other arithmetic  1.74 us (1%)
    ppermute x34, waiting for transfers between devices, send(): return lax.ppermute(value, 'fsdp', pairs)  57.8 us
    ppermute x34, starting transfers between devices, send(): return lax.ppermute(value, 'fsdp', pairs)  39 us
    pallas_call x3, Pallas kernels, call(): pl.pallas_call(kernel, in_specs=[spec for spec, _ in ins], out_specs=[spe...  26.9 us
    unnamed x33, local copies, waits for them, and re-layouts  9.21 us
    ppermute x1, waiting for transfers between devices, body(): other_query = lax.ppermute(query_all, 'dp', SENT)  6.91 us
  transfers between devices with their start and end apart: 36, of which 21 were waited for; matrix products, arithmetic and copies ran while one was open for 3% of the time, Pallas kernels for 3%

profile of v2, /device:TPU:6, one launch (start us, length us, event | category | flops | bytes accessed | tf_op | source)
XLA Modules:
  0.0 153.9 jit_solution(10995097634259845401)
XLA Ops:
  3.0 0.9 collective-permute-start
  4.2 3.3 %collective-permute-done = bf16[2,19200]{1,0:T(2,128)(2,1)S(1)} collective-permute-done((bf16[2,19200]{1,0:T(2,128)(2,1)S(1)}, bf16[2,19200]{1,0:T(2,128)(2,1)S(1)}, u32[]{:S(2)}, u32[]{:S(2)}) %collective-permute-start) | collective-permute-done | bytes 76832 | tf_op jit(solution)/shard_map/ppermute | solution.py:48
  7.5 2.0 %collective-permute-start.1 = (bf16[2,2,19200]{2,1,0:T(2,128)(2,1)S(1)}, bf16[2,2,19200]{2,1,0:T(2,128)(2,1)S(1)}, u32[]{:S(2)}, u32[]{:S(2)}) collective-permute-start(bf16[2,2,19200]{2,1,0:T(2,128)(2,1)S(1)} %bitcast_dynamic-update-slice_fusion.6), channel_id=1, source_target_pairs={{0,16},{2,6},{4,20},{6,10},{8,24},{10,14},{12,28},{14,2},{16,32},{... | collective-permute-start | bytes 460808 | tf_op jit(solution)/shard_map/ppermute | solution.py:48
  9.5 3.6 %collective-permute-start.2 = (bf16[2,2,19200]{2,1,0:T(2,128)(2,1)S(1)}, bf16[2,2,19200]{2,1,0:T(2,128)(2,1)S(1)}, u32[]{:S(2)}, u32[]{:S(2)}) collective-permute-start(bf16[2,2,19200]{2,1,0:T(2,128)(2,1)S(1)} %bitcast_dynamic-update-slice_fusion.6), channel_id=1, source_target_pairs={{0,32},{2,10},{4,36},{6,14},{8,40},{10,2},{12,44},{14,6},{16,48},{... | collective-permute-start | bytes 460808 | tf_op jit(solution)/shard_map/ppermute | solution.py:48
  13.1 1.0 collective-permute-start.3
  14.9 3.0 %collective-permute-done.2 = bf16[2,2,19200]{2,1,0:T(2,128)(2,1)S(1)} collective-permute-done((bf16[2,2,19200]{2,1,0:T(2,128)(2,1)S(1)}, bf16[2,2,19200]{2,1,0:T(2,128)(2,1)S(1)}, u32[]{:S(2)}, u32[]{:S(2)}) %collective-permute-start.2) | collective-permute-done | bytes 153632 | tf_op jit(solution)/shard_map/ppermute | solution.py:48
  18.7 3.3 %collective-permute-start.4 = (bf16[16,19200]{1,0:T(8,128)(2,1)S(1)}, bf16[16,19200]{1,0:T(8,128)(2,1)S(1)}, u32[]{:S(2)}, u32[]{:S(2)}) collective-permute-start(bf16[16,19200]{1,0:T(8,128)(2,1)S(1)} %reshape.26.refs_0_), channel_id=1, source_target_pairs={{0,8},{2,34},{4,12},{6,38},{8,0},{10,42},{12,4},{14,46},{16,24},{1... | collective-permute-start | bytes 1843208 | tf_op jit(solution)/shard_map/ppermute | solution.py:48
  22.6 2.6 %collective-permute-start.6 = (bf16[16,19200]{1,0:T(8,128)(2,1)S(1)}, bf16[16,19200]{1,0:T(8,128)(2,1)S(1)}, u32[]{:S(2)}, u32[]{:S(2)}) collective-permute-start(bf16[16,19200]{1,0:T(8,128)(2,1)S(1)} %reshape.26.refs_0_), channel_id=1, source_target_pairs={{0,12},{2,50},{4,0},{6,54},{8,4},{10,58},{12,8},{14,62},{16,28},{1... | collective-permute-start | bytes 1843208 | tf_op jit(solution)/shard_map/ppermute | solution.py:48
  25.2 5.3 %collective-permute-done.4.refs_2_ = bf16[16,19200]{1,0:T(8,128)(2,1)S(1)} collective-permute-done((bf16[16,19200]{1,0:T(8,128)(2,1)S(1)}, bf16[16,19200]{1,0:T(8,128)(2,1)S(1)}, u32[]{:S(2)}, u32[]{:S(2)}) %collective-permute-start.4) | collective-permute-done | bytes 614432 | tf_op jit(solution)/shard_map/ppermute | solution.py:48
  30.5 6.5 %collective-permute-done.5.refs_1_ = bf16[16,19200]{1,0:T(8,128)(2,1)S(1)} collective-permute-done((bf16[16,19200]{1,0:T(8,128)(2,1)S(1)}, bf16[16,19200]{1,0:T(8,128)(2,1)S(1)}, u32[]{:S(2)}, u32[]{:S(2)}) %collective-permute-start.5) | collective-permute-done | bytes 614432 | tf_op jit(solution)/shard_map/ppermute | solution.py:48
  38.5 2.8 %collective-permute-done.7 = bf16[64,768]{1,0:T(8,128)(2,1)S(1)} collective-permute-done((bf16[64,768]{1,0:T(8,128)(2,1)S(1)}, bf16[64,768]{1,0:T(8,128)(2,1)S(1)}, u32[]{:S(2)}, u32[]{:S(2)}) %collective-permute-start.7) | collective-permute-done | bytes 98336 | tf_op jit(solution)/shard_map/ppermute | solution.py:48
  41.6 0.9 collective-permute-start.8
  42.5 3.1 %collective-permute-done.8 = bf16[144,128]{1,0:T(8,128)(2,1)S(1)} collective-permute-done((bf16[144,128]{1,0:T(8,128)(2,1)S(1)}, bf16[144,128]{1,0:T(8,128)(2,1)S(1)}, u32[]{:S(2)}, u32[]{:S(2)}) %collective-permute-start.8) | collective-permute-done | bytes 36896 | tf_op jit(solution)/shard_map/ppermute | solution.py:48
  45.6 0.8 copy-done.1
  46.5 0.9 copy-done.3
  47.3 0.8 copy-done.5
  48.1 2.1 %collective-permute-start.13 = (bf16[288,128]{1,0:T(8,128)(2,1)S(1)}, bf16[288,128]{1,0:T(8,128)(2,1)S(1)}, u32[]{:S(2)}, u32[]{:S(2)}) collective-permute-start(bf16[288,128]{1,0:T(8,128)(2,1)S(1)} %pad_maximum_fusion), channel_id=1, source_target_pairs={{0,32},{2,10},{4,36},{6,14},{8,40},{10,2},{12,44},{14,6},{16,48},{... | collective-permute-start | bytes 221192 | tf_op jit(solution)/shard_map/ppermute | solution.py:48
  50.3 0.9 collective-permute-start.14
  51.2 2.3 %collective-permute-start.15 = (bf16[288,128]{1,0:T(8,128)(2,1)S(1)}, bf16[288,128]{1,0:T(8,128)(2,1)S(1)}, u32[]{:S(2)}, u32[]{:S(2)}) collective-permute-start(bf16[288,128]{1,0:T(8,128)(2,1)S(1)} %pad_maximum_fusion), channel_id=1, source_target_pairs={{0,48},{2,14},{4,52},{6,2},{8,56},{10,6},{12,60},{14,10},{16,0},{1... | collective-permute-start | bytes 221192 | tf_op jit(solution)/shard_map/ppermute | solution.py:48
  54.2 1.7 %collective-permute-done.14 = bf16[288,128]{1,0:T(8,128)(2,1)S(1)} collective-permute-done((bf16[288,128]{1,0:T(8,128)(2,1)S(1)}, bf16[288,128]{1,0:T(8,128)(2,1)S(1)}, u32[]{:S(2)}, u32[]{:S(2)}) %collective-permute-start.14) | collective-permute-done | bytes 73760 | tf_op jit(solution)/shard_map/ppermute | solution.py:48
  57.8 2.0 %collective-permute-start.16 = (bf16[1152,128]{1,0:T(8,128)(2,1)}, bf16[1152,128]{1,0:T(8,128)(2,1)}, u32[]{:S(2)}, u32[]{:S(2)}) collective-permute-start(bf16[1152,128]{1,0:T(8,128)(2,1)} %constant_dynamic-update-slice_fusion.3.refs_0_), channel_id=1, source_target_pairs={{0,8},{2,34},{4,12},{6,38},{8,0},{10,42},{12,4},{14,46},{16,24},{1... | collective-permute-start | bytes 884744 | tf_op jit(solution)/shard_map/ppermute | solution.py:48
  59.8 1.5 collective-permute-start.17
  61.3 1.8 %collective-permute-start.18 = (bf16[1152,128]{1,0:T(8,128)(2,1)}, bf16[1152,128]{1,0:T(8,128)(2,1)}, u32[]{:S(2)}, u32[]{:S(2)}) collective-permute-start(bf16[1152,128]{1,0:T(8,128)(2,1)} %constant_dynamic-update-slice_fusion.3.refs_0_), channel_id=1, source_target_pairs={{0,12},{2,50},{4,0},{6,54},{8,4},{10,58},{12,8},{14,62},{16,28},{1... | collective-permute-start | bytes 884744 | tf_op jit(solution)/shard_map/ppermute | solution.py:48
  63.0 3.4 %collective-permute-done.16.refs_2_ = bf16[1152,128]{1,0:T(8,128)(2,1)} collective-permute-done((bf16[1152,128]{1,0:T(8,128)(2,1)}, bf16[1152,128]{1,0:T(8,128)(2,1)}, u32[]{:S(2)}, u32[]{:S(2)}) %collective-permute-start.16) | collective-permute-done | bytes 294944 | tf_op jit(solution)/shard_map/ppermute | solution.py:48
  66.4 3.1 %collective-permute-done.17.refs_1_ = bf16[1152,128]{1,0:T(8,128)(2,1)} collective-permute-done((bf16[1152,128]{1,0:T(8,128)(2,1)}, bf16[1152,128]{1,0:T(8,128)(2,1)}, u32[]{:S(2)}, u32[]{:S(2)}) %collective-permute-start.17) | collective-permute-done | bytes 294944 | tf_op jit(solution)/shard_map/ppermute | solution.py:48
  70.1 1.1 copy-done.2
  71.2 1.1 copy-done.4
  72.3 1.1 copy-done.6
  73.3 4.3 %shard_map.138 = (bf16[128,9216]{1,0:T(8,128)(2,1)S(1)}, bf16[128,9216]{1,0:T(8,128)(2,1)S(1)}, f32[144,128]{1,0:T(8,128)S(1)}, bf16[16,9216]{1,0:T(8,128)(2,1)S(1)}) custom-call(s32[5]{0:T(128)S(1)} %stack.23.place, bf16[16,19200]{1,0:T(8,128)(2,1)S(1)} %reshape.26.refs_0_, bf16[16,19200]{1,0:T(8,128)(2,1)S(1)} %collective-permute-done.5.refs_1_, ...), custom_call_target="tpu_custom_call" | custom-call | bytes 18450000 | tf_op jit(solution)/shard_map/pallas_call | solution.py:328
  77.7 20.5 %shard_map.139 = (bf16[3584,128]{1,0:T(8,128)(2,1)S(1)}, bf16[3584,128]{1,0:T(8,128)(2,1)S(1)}, bf16[3584,128]{1,0:T(8,128)(2,1)S(1)}, bf16[3584,128]{1,0:T(8,12...) custom-call(s32[5]{0:T(128)S(1)} %stack.23.place, ...), custom_call_target="tpu_custom_call" | custom-call | bytes 73800000 | tf_op jit(solution)/shard_map/pallas_call | solution.py:328
  99.3 1.5 collective-permute-done.27
  101.1 2.1 %collective-permute-start.28 = (bf16[3584,128]{1,0:T(8,128)(2,1)S(1)}, bf16[3584,128]{1,0:T(8,128)(2,1)S(1)}, u32[]{:S(2)}, u32[]{:S(2)}) collective-permute-start(bf16[3584,128]{1,0:T(8,128)(2,1)S(1)} %add_convert_fusion), channel_id=1, source_target_pairs={{0,8},{2,34},{4,12},{6,38},{8,0},{10,42},{12,4},{14,46},{16,24},{1... | collective-permute-start | bytes 2752520 | tf_op jit(solution)/shard_map/ppermute | solution.py:48
  103.4 1.5 collective-permute-start.26
  105.2 1.9 %collective-permute-start.24 = (bf16[3584,128]{1,0:T(8,128)(2,1)S(1)}, bf16[3584,128]{1,0:T(8,128)(2,1)S(1)}, u32[]{:S(2)}, u32[]{:S(2)}) collective-permute-start(bf16[3584,128]{1,0:T(8,128)(2,1)S(1)} %add_convert_fusion.2), channel_id=1, source_target_pairs={{0,12},{2,50},{4,0},{6,54},{8,4},{10,58},{12,8},{14,62},{16,28},{1... | collective-permute-start | bytes 2752520 | tf_op jit(solution)/shard_map/ppermute | solution.py:48
  107.1 1.4 collective-permute-start.30
  108.5 6.9 %collective-permute-done.30.refs_5_ = bf16[128,768]{1,0:T(8,128)(2,1)S(1)} collective-permute-done((bf16[128,768]{1,0:T(8,128)(2,1)S(1)}, bf16[128,768]{1,0:T(8,128)(2,1)S(1)}, u32[]{:S(2)}, u32[]{:S(2)}) %collective-permute-start.30) | collective-permute-done | bytes 196640 | tf_op jit(solution)/shard_map/ppermute | solution.py:387
  116.2 9.7 %collective-permute-done.26.refs_2_ = bf16[3584,128]{1,0:T(8,128)(2,1)S(1)} collective-permute-done((bf16[3584,128]{1,0:T(8,128)(2,1)S(1)}, bf16[3584,128]{1,0:T(8,128)(2,1)S(1)}, u32[]{:S(2)}, u32[]{:S(2)}) %collective-permute-start.26) | collective-permute-done | bytes 917536 | tf_op jit(solution)/shard_map/ppermute | solution.py:48
  125.9 2.1 %shard_map.140 = (f32[2,448,128]{2,1,0:T(8,128)S(1)}, bf16[2,448,128]{2,1,0:T(8,128)(2,1)S(1)}, bf16[2,448,128]{2,1,0:T(8,128)(2,1)S(1)}, bf16[2,448,128]{2,1,0:T(8,128)(2,1)S(1)}) custom-call(s32[5]{0:T(128)S(1)} %stack.23.place, bf16[3584,128]{1,0:T(8,128)(2,1)S(1)} %get-tuple-element.63.refs_0_, bf16[3584,128]{1,0:T(8,128)(2,1)S(1)} %collective-permute-done.24.refs_1_, ...), custom_call_target="tpu_custom_call" | custom-call | bytes 11070000 | tf_op jit(solution)/shard_map/pallas_call | solution.py:328
  128.0 3.3 %collective-permute-start.31 = (bf16[2,448,128]{2,1,0:T(8,128)(2,1)S(1)}, bf16[2,448,128]{2,1,0:T(8,128)(2,1)S(1)}, u32[]{:S(2)}, u32[]{:S(2)}) collective-permute-start(bf16[2,448,128]{2,1,0:T(8,128)(2,1)S(1)} %get-tuple-element.72), channel_id=1, source_target_pairs={{0,48},{2,14},{4,52},{6,2},{8,56},{10,6},{12,60},{14,10},{16,0},{1... | collective-permute-start | bytes 688136 | tf_op jit(solution)/shard_map/ppermute | solution.py:48
  131.3 0.9 collective-permute-start.33
  132.3 5.0 %collective-permute-done.31 = bf16[2,448,128]{2,1,0:T(8,128)(2,1)S(1)} collective-permute-done((bf16[2,448,128]{2,1,0:T(8,128)(2,1)S(1)}, bf16[2,448,128]{2,1,0:T(8,128)(2,1)S(1)}, u32[]{:S(2)}, u32[]{:S(2)}) %collective-permute-start.31) | collective-permute-done | bytes 229408 | tf_op jit(solution)/shard_map/ppermute | solution.py:48
  137.3 1.6 %collective-permute-done.32 = bf16[2,448,128]{2,1,0:T(8,128)(2,1)S(1)} collective-permute-done((bf16[2,448,128]{2,1,0:T(8,128)(2,1)S(1)}, bf16[2,448,128]{2,1,0:T(8,128)(2,1)S(1)}, u32[]{:S(2)}, u32[]{:S(2)}) %collective-permute-start.32) | collective-permute-done | bytes 229408 | tf_op jit(solution)/shard_map/ppermute | solution.py:48
  138.9 2.1 %collective-permute-done.33 = bf16[2,448,128]{2,1,0:T(8,128)(2,1)S(1)} collective-permute-done((bf16[2,448,128]{2,1,0:T(8,128)(2,1)S(1)}, bf16[2,448,128]{2,1,0:T(8,128)(2,1)S(1)}, u32[]{:S(2)}, u32[]{:S(2)}) %collective-permute-start.33) | collective-permute-done | bytes 229408 | tf_op jit(solution)/shard_map/ppermute | solution.py:48
  141.1 0.9 collective-permute-start.34
  142.1 4.2 %collective-permute-done.34 = bf16[448,128]{1,0:T(8,128)(2,1)S(1)} collective-permute-done((bf16[448,128]{1,0:T(8,128)(2,1)S(1)}, bf16[448,128]{1,0:T(8,128)(2,1)S(1)}, u32[]{:S(2)}, u32[]{:S(2)}) %collective-permute-start.34) | collective-permute-done | bytes 114720 | tf_op jit(solution)/shard_map/ppermute | solution.py:48
  146.5 1.2 collective-permute-start.35
  149.0 3.0 %collective-permute-done.35 = bf16[144,128]{1,0:T(8,128)(2,1)S(1)} collective-permute-done((bf16[144,128]{1,0:T(8,128)(2,1)S(1)}, bf16[144,128]{1,0:T(8,128)(2,1)S(1)}, u32[]{:S(2)}, u32[]{:S(2)}) %collective-permute-start.35) | collective-permute-done | bytes 36896 | tf_op jit(solution)/shard_map/ppermute | solution.py:472
  152.3 1.0 convolution_add_fusion
  (102 shorter events, 15.1 us)
Async XLA Ops:
  0.6 40.7 %copy-start = (bf16[768,144]{0,1:T(8,128)(2,1)S(1)}, bf16[768,144]{0,1:T(8,128)(2,1)}, u32[]{:S(2)}) copy-start(bf16[768,144]{0,1:T(8,128)(2,1)} %param.12) | copy-start | bytes 663556
  3.0 4.5 %collective-permute-start = (bf16[2,19200]{1,0:T(2,128)(2,1)S(1)}, bf16[2,19200]{1,0:T(2,128)(2,1)S(1)}, u32[]{:S(2)}, u32[]{:S(2)}) collective-permute-start(bf16[2,19200]{1,0:T(2,128)(2,1)S(1)} %constant_dynamic-update-slice_fusion), channel_id=1, source_target_pairs={{0,64},{2,66},{4,68},{6,70},{8,72},{10,74},{12,76},{14,78},{16,80}... | collective-permute-start | bytes 230408 | tf_op jit(solution)/shard_map/ppermute | solution.py:48
  4.0 21.2 %copy-start.13 = (bf16[144]{0:T(256)(128)(2,1)S(1)}, bf16[144]{0:T(256)(128)(2,1)}, u32[]{:S(2)}) copy-start(bf16[144]{0:T(256)(128)(2,1)} %param.13) | copy-start | bytes 868
  7.5 7.3 %collective-permute-start.1 = (bf16[2,2,19200]{2,1,0:T(2,128)(2,1)S(1)}, bf16[2,2,19200]{2,1,0:T(2,128)(2,1)S(1)}, u32[]{:S(2)}, u32[]{:S(2)}) collective-permute-start(bf16[2,2,19200]{2,1,0:T(2,128)(2,1)S(1)} %bitcast_dynamic-update-slice_fusion.6), channel_id=1, source_target_pairs={{0,16},{2,6},{4,20},{6,10},{8,24},{10,14},{12,28},{14,2},{16,32},{... | collective-permute-start | bytes 460808 | tf_op jit(solution)/shard_map/ppermute | solution.py:48
  9.5 8.4 %collective-permute-start.2 = (bf16[2,2,19200]{2,1,0:T(2,128)(2,1)S(1)}, bf16[2,2,19200]{2,1,0:T(2,128)(2,1)S(1)}, u32[]{:S(2)}, u32[]{:S(2)}) collective-permute-start(bf16[2,2,19200]{2,1,0:T(2,128)(2,1)S(1)} %bitcast_dynamic-update-slice_fusion.6), channel_id=1, source_target_pairs={{0,32},{2,10},{4,36},{6,14},{8,40},{10,2},{12,44},{14,6},{16,48},{... | collective-permute-start | bytes 460808 | tf_op jit(solution)/shard_map/ppermute | solution.py:48
  13.1 5.2 %collective-permute-start.3 = (bf16[2,2,19200]{2,1,0:T(2,128)(2,1)S(1)}, bf16[2,2,19200]{2,1,0:T(2,128)(2,1)S(1)}, u32[]{:S(2)}, u32[]{:S(2)}) collective-permute-start(bf16[2,2,19200]{2,1,0:T(2,128)(2,1)S(1)} %bitcast_dynamic-update-slice_fusion.6), channel_id=1, source_target_pairs={{0,48},{2,14},{4,52},{6,2},{8,56},{10,6},{12,60},{14,10},{16,0},{1... | collective-permute-start | bytes 460808 | tf_op jit(solution)/shard_map/ppermute | solution.py:48
  18.0 51.9 %copy-start.12 = (bf16[576]{0:T(1024)(128)(2,1)S(1)}, bf16[576]{0:T(1024)(128)(2,1)}, u32[]{:S(2)}) copy-start(bf16[576]{0:T(1024)(128)(2,1)} %param.18) | copy-start | bytes 3460
  18.1 52.0 %copy-start.7 = (f32[9216]{0:T(1024)S(1)}, f32[9216]{0:T(1024)}, u32[]{:S(2)}) copy-start(f32[9216]{0:T(1024)} %param.15) | copy-start | bytes 110596
  18.1 52.0 %copy-start.8 = (f32[9216]{0:T(1024)S(1)}, f32[9216]{0:T(1024)}, u32[]{:S(2)}) copy-start(f32[9216]{0:T(1024)} %param.16) | copy-start | bytes 110596
  18.7 11.8 %collective-permute-start.4 = (bf16[16,19200]{1,0:T(8,128)(2,1)S(1)}, bf16[16,19200]{1,0:T(8,128)(2,1)S(1)}, u32[]{:S(2)}, u32[]{:S(2)}) collective-permute-start(bf16[16,19200]{1,0:T(8,128)(2,1)S(1)} %reshape.26.refs_0_), channel_id=1, source_target_pairs={{0,8},{2,34},{4,12},{6,38},{8,0},{10,42},{12,4},{14,46},{16,24},{1... | collective-permute-start | bytes 1843208 | tf_op jit(solution)/shard_map/ppermute | solution.py:48
  21.9 15.0 %collective-permute-start.5 = (bf16[16,19200]{1,0:T(8,128)(2,1)S(1)}, bf16[16,19200]{1,0:T(8,128)(2,1)S(1)}, u32[]{:S(2)}, u32[]{:S(2)}) collective-permute-start(bf16[16,19200]{1,0:T(8,128)(2,1)S(1)} %reshape.26.refs_0_), channel_id=1, source_target_pairs={{0,4},{2,18},{4,8},{6,22},{8,12},{10,26},{12,0},{14,30},{16,20},{1... | collective-permute-start | bytes 1843208 | tf_op jit(solution)/shard_map/ppermute | solution.py:48
  22.6 14.7 %collective-permute-start.6 = (bf16[16,19200]{1,0:T(8,128)(2,1)S(1)}, bf16[16,19200]{1,0:T(8,128)(2,1)S(1)}, u32[]{:S(2)}, u32[]{:S(2)}) collective-permute-start(bf16[16,19200]{1,0:T(8,128)(2,1)S(1)} %reshape.26.refs_0_), channel_id=1, source_target_pairs={{0,12},{2,50},{4,0},{6,54},{8,4},{10,58},{12,8},{14,62},{16,28},{1... | collective-permute-start | bytes 1843208 | tf_op jit(solution)/shard_map/ppermute | solution.py:48
  25.2 20.4 %collective-permute-start.9 = (bf16[16,19200]{1,0:T(8,128)(2,1)S(1)}, bf16[16,19200]{1,0:T(8,128)(2,1)S(1)}, u32[]{:S(2)}, u32[]{:S(2)}) collective-permute-start(bf16[16,19200]{1,0:T(8,128)(2,1)S(1)} %reshape.26.refs_0_), channel_id=1, source_target_pairs={{0,2},{2,0},{4,6},{6,4},{8,10},{10,8},{12,14},{14,12},{16,18},{18,... | collective-permute-start | bytes 1843208 | tf_op jit(solution)/shard_map/ppermute | solution.py:48
  37.4 8.3 %collective-permute-start.10 = (bf16[16,19200]{1,0:T(8,128)(2,1)S(1)}, bf16[16,19200]{1,0:T(8,128)(2,1)S(1)}, u32[]{:S(2)}, u32[]{:S(2)}) collective-permute-start(bf16[16,19200]{1,0:T(8,128)(2,1)S(1)} %collective-permute-done.5.refs_1_), channel_id=1, source_target_pairs={{0,2},{2,0},{4,6},{6,4},{8,10},{10,8},{12,14},{14,12},{16,18},{18,... | collective-permute-start | bytes 1843208 | tf_op jit(solution)/shard_map/ppermute | solution.py:48
  37.4 9.1 %collective-permute-start.11 = (bf16[16,19200]{1,0:T(8,128)(2,1)S(1)}, bf16[16,19200]{1,0:T(8,128)(2,1)S(1)}, u32[]{:S(2)}, u32[]{:S(2)}) collective-permute-start(bf16[16,19200]{1,0:T(8,128)(2,1)S(1)} %collective-permute-done.4.refs_2_), channel_id=1, source_target_pairs={{0,2},{2,0},{4,6},{6,4},{8,10},{10,8},{12,14},{14,12},{16,18},{18,... | collective-permute-start | bytes 1843208 | tf_op jit(solution)/shard_map/ppermute | solution.py:48
  37.9 9.5 %collective-permute-start.12 = (bf16[16,19200]{1,0:T(8,128)(2,1)S(1)}, bf16[16,19200]{1,0:T(8,128)(2,1)S(1)}, u32[]{:S(2)}, u32[]{:S(2)}) collective-permute-start(bf16[16,19200]{1,0:T(8,128)(2,1)S(1)} %collective-permute-done.6.refs_3_), channel_id=1, source_target_pairs={{0,2},{2,0},{4,6},{6,4},{8,10},{10,8},{12,14},{14,12},{16,18},{18,... | collective-permute-start | bytes 1843208 | tf_op jit(solution)/shard_map/ppermute | solution.py:48
  37.9 3.4 %collective-permute-start.7 = (bf16[64,768]{1,0:T(8,128)(2,1)S(1)}, bf16[64,768]{1,0:T(8,128)(2,1)S(1)}, u32[]{:S(2)}, u32[]{:S(2)}) collective-permute-start(bf16[64,768]{1,0:T(8,128)(2,1)S(1)} %bitcast.69), channel_id=1, source_target_pairs={{0,2},{2,0},{4,6},{6,4},{8,10},{10,8},{12,14},{14,12},{16,18},{18,... | collective-permute-start | bytes 294920 | tf_op jit(solution)/shard_map/ppermute | solution.py:48
  41.3 28.7 %copy-start.10 = (bf16[2,64,768]{2,1,0:T(8,128)(2,1)}, bf16[2,64,768]{2,1,0:T(8,128)(2,1)S(1)}, u32[]{:S(2)}) copy-start(bf16[2,64,768]{2,1,0:T(8,128)(2,1)S(1)} %bitcast_dynamic-update-slice_fusion.4) | copy-start | bytes 589828
  41.6 4.0 %collective-permute-start.8 = (bf16[144,128]{1,0:T(8,128)(2,1)S(1)}, bf16[144,128]{1,0:T(8,128)(2,1)S(1)}, u32[]{:S(2)}, u32[]{:S(2)}) collective-permute-start(bf16[144,128]{1,0:T(8,128)(2,1)S(1)} %fusion.1), channel_id=1, source_target_pairs={{0,64},{2,66},{4,68},{6,70},{8,72},{10,74},{12,76},{14,78},{16,80}... | collective-permute-start | bytes 110600 | tf_op jit(solution)/shard_map/ppermute | solution.py:48
  46.5 0.9 copy-start.3
  48.1 6.0 %collective-permute-start.13 = (bf16[288,128]{1,0:T(8,128)(2,1)S(1)}, bf16[288,128]{1,0:T(8,128)(2,1)S(1)}, u32[]{:S(2)}, u32[]{:S(2)}) collective-permute-start(bf16[288,128]{1,0:T(8,128)(2,1)S(1)} %pad_maximum_fusion), channel_id=1, source_target_pairs={{0,32},{2,10},{4,36},{6,14},{8,40},{10,2},{12,44},{14,6},{16,48},{... | collective-permute-start | bytes 221192 | tf_op jit(solution)/shard_map/ppermute | solution.py:48
  50.3 5.6 %collective-permute-start.14 = (bf16[288,128]{1,0:T(8,128)(2,1)S(1)}, bf16[288,128]{1,0:T(8,128)(2,1)S(1)}, u32[]{:S(2)}, u32[]{:S(2)}) collective-permute-start(bf16[288,128]{1,0:T(8,128)(2,1)S(1)} %pad_maximum_fusion), channel_id=1, source_target_pairs={{0,16},{2,6},{4,20},{6,10},{8,24},{10,14},{12,28},{14,2},{16,32},{... | collective-permute-start | bytes 221192 | tf_op jit(solution)/shard_map/ppermute | solution.py:48
  51.2 4.6 %collective-permute-start.15 = (bf16[288,128]{1,0:T(8,128)(2,1)S(1)}, bf16[288,128]{1,0:T(8,128)(2,1)S(1)}, u32[]{:S(2)}, u32[]{:S(2)}) collective-permute-start(bf16[288,128]{1,0:T(8,128)(2,1)S(1)} %pad_maximum_fusion), channel_id=1, source_target_pairs={{0,48},{2,14},{4,52},{6,2},{8,56},{10,6},{12,60},{14,10},{16,0},{1... | collective-permute-start | bytes 221192 | tf_op jit(solution)/shard_map/ppermute | solution.py:48
  57.8 8.6 %collective-permute-start.16 = (bf16[1152,128]{1,0:T(8,128)(2,1)}, bf16[1152,128]{1,0:T(8,128)(2,1)}, u32[]{:S(2)}, u32[]{:S(2)}) collective-permute-start(bf16[1152,128]{1,0:T(8,128)(2,1)} %constant_dynamic-update-slice_fusion.3.refs_0_), channel_id=1, source_target_pairs={{0,8},{2,34},{4,12},{6,38},{8,0},{10,42},{12,4},{14,46},{16,24},{1... | collective-permute-start | bytes 884744 | tf_op jit(solution)/shard_map/ppermute | solution.py:48
  59.8 9.7 %collective-permute-start.17 = (bf16[1152,128]{1,0:T(8,128)(2,1)}, bf16[1152,128]{1,0:T(8,128)(2,1)}, u32[]{:S(2)}, u32[]{:S(2)}) collective-permute-start(bf16[1152,128]{1,0:T(8,128)(2,1)} %constant_dynamic-update-slice_fusion.3.refs_0_), channel_id=1, source_target_pairs={{0,4},{2,18},{4,8},{6,22},{8,12},{10,26},{12,0},{14,30},{16,20},{1... | collective-permute-start | bytes 884744 | tf_op jit(solution)/shard_map/ppermute | solution.py:48
  61.3 8.2 %collective-permute-start.18 = (bf16[1152,128]{1,0:T(8,128)(2,1)}, bf16[1152,128]{1,0:T(8,128)(2,1)}, u32[]{:S(2)}, u32[]{:S(2)}) collective-permute-start(bf16[1152,128]{1,0:T(8,128)(2,1)} %constant_dynamic-update-slice_fusion.3.refs_0_), channel_id=1, source_target_pairs={{0,12},{2,50},{4,0},{6,54},{8,4},{10,58},{12,8},{14,62},{16,28},{1... | collective-permute-start | bytes 884744 | tf_op jit(solution)/shard_map/ppermute | solution.py:48
  63.0 14.6 %collective-permute-start.19 = (bf16[1152,128]{1,0:T(8,128)(2,1)}, bf16[1152,128]{1,0:T(8,128)(2,1)}, u32[]{:S(2)}, u32[]{:S(2)}) collective-permute-start(bf16[1152,128]{1,0:T(8,128)(2,1)} %constant_dynamic-update-slice_fusion.3.refs_0_), channel_id=1, source_target_pairs={{0,2},{2,0},{4,6},{6,4},{8,10},{10,8},{12,14},{14,12},{16,18},{18,... | collective-permute-start | bytes 884744 | tf_op jit(solution)/shard_map/ppermute | solution.py:48
  69.5 8.2 %collective-permute-start.20 = (bf16[1152,128]{1,0:T(8,128)(2,1)}, bf16[1152,128]{1,0:T(8,128)(2,1)}, u32[]{:S(2)}, u32[]{:S(2)}) collective-permute-start(bf16[1152,128]{1,0:T(8,128)(2,1)} %collective-permute-done.17.refs_1_), channel_id=1, source_target_pairs={{0,2},{2,0},{4,6},{6,4},{8,10},{10,8},{12,14},{14,12},{16,18},{18,... | collective-permute-start | bytes 884744 | tf_op jit(solution)/shard_map/ppermute | solution.py:48
  69.5 8.2 %collective-permute-start.21 = (bf16[1152,128]{1,0:T(8,128)(2,1)}, bf16[1152,128]{1,0:T(8,128)(2,1)}, u32[]{:S(2)}, u32[]{:S(2)}) collective-permute-start(bf16[1152,128]{1,0:T(8,128)(2,1)} %collective-permute-done.16.refs_2_), channel_id=1, source_target_pairs={{0,2},{2,0},{4,6},{6,4},{8,10},{10,8},{12,14},{14,12},{16,18},{18,... | collective-permute-start | bytes 884744 | tf_op jit(solution)/shard_map/ppermute | solution.py:48
  70.0 7.7 %collective-permute-start.22 = (bf16[1152,128]{1,0:T(8,128)(2,1)}, bf16[1152,128]{1,0:T(8,128)(2,1)}, u32[]{:S(2)}, u32[]{:S(2)}) collective-permute-start(bf16[1152,128]{1,0:T(8,128)(2,1)} %collective-permute-done.18.refs_3_), channel_id=1, source_target_pairs={{0,2},{2,0},{4,6},{6,4},{8,10},{10,8},{12,14},{14,12},{16,18},{18,... | collective-permute-start | bytes 884744 | tf_op jit(solution)/shard_map/ppermute | solution.py:48
  70.1 1.1 copy-start.2
  71.2 1.1 copy-start.4
  72.2 1.1 copy-start.6
  73.3 4.3 %copy-start.9 = (f32[9216]{0:T(1024)S(1)}, f32[9216]{0:T(1024)}, u32[]{:S(2)}) copy-start(f32[9216]{0:T(1024)} %param.20) | copy-start | bytes 110596
  98.2 2.7 %collective-permute-start.27 = (bf16[3584,128]{1,0:T(8,128)(2,1)S(1)}, bf16[3584,128]{1,0:T(8,128)(2,1)S(1)}, u32[]{:S(2)}, u32[]{:S(2)}) collective-permute-start(bf16[3584,128]{1,0:T(8,128)(2,1)S(1)} %get-tuple-element.69), channel_id=1, source_target_pairs={{0,2},{2,0},{4,6},{6,4},{8,10},{10,8},{12,14},{14,12},{16,18},{18,... | collective-permute-start | bytes 2752520 | tf_op jit(solution)/shard_map/ppermute | solution.py:48
  98.7 4.5 %collective-permute-start.25 = (bf16[3584,128]{1,0:T(8,128)(2,1)S(1)}, bf16[3584,128]{1,0:T(8,128)(2,1)S(1)}, u32[]{:S(2)}, u32[]{:S(2)}) collective-permute-start(bf16[3584,128]{1,0:T(8,128)(2,1)S(1)} %get-tuple-element.67), channel_id=1, source_target_pairs={{0,2},{2,0},{4,6},{6,4},{8,10},{10,8},{12,14},{14,12},{16,18},{18,... | collective-permute-start | bytes 2752520 | tf_op jit(solution)/shard_map/ppermute | solution.py:48
  98.8 6.1 %collective-permute-start.23 = (bf16[3584,128]{1,0:T(8,128)(2,1)S(1)}, bf16[3584,128]{1,0:T(8,128)(2,1)S(1)}, u32[]{:S(2)}, u32[]{:S(2)}) collective-permute-start(bf16[3584,128]{1,0:T(8,128)(2,1)S(1)} %get-tuple-element.65), channel_id=1, source_target_pairs={{0,2},{2,0},{4,6},{6,4},{8,10},{10,8},{12,14},{14,12},{16,18},{18,... | collective-permute-start | bytes 2752520 | tf_op jit(solution)/shard_map/ppermute | solution.py:48
  99.2 16.1 %collective-permute-start.29 = (bf16[3584,128]{1,0:T(8,128)(2,1)S(1)}, bf16[3584,128]{1,0:T(8,128)(2,1)S(1)}, u32[]{:S(2)}, u32[]{:S(2)}) collective-permute-start(bf16[3584,128]{1,0:T(8,128)(2,1)S(1)} %get-tuple-element.70), channel_id=1, source_target_pairs={{0,2},{2,0},{4,6},{6,4},{8,10},{10,8},{12,14},{14,12},{16,18},{18,... | collective-permute-start | bytes 2752520 | tf_op jit(solution)/shard_map/ppermute | solution.py:48
  101.1 15.1 %collective-permute-start.28 = (bf16[3584,128]{1,0:T(8,128)(2,1)S(1)}, bf16[3584,128]{1,0:T(8,128)(2,1)S(1)}, u32[]{:S(2)}, u32[]{:S(2)}) collective-permute-start(bf16[3584,128]{1,0:T(8,128)(2,1)S(1)} %add_convert_fusion), channel_id=1, source_target_pairs={{0,8},{2,34},{4,12},{6,38},{8,0},{10,42},{12,4},{14,46},{16,24},{1... | collective-permute-start | bytes 2752520 | tf_op jit(solution)/shard_map/ppermute | solution.py:48
  103.4 3.6 %copy-start.11 = (bf16[2,64,768]{2,1,0:T(8,128)(2,1)S(1)}, bf16[2,64,768]{2,1,0:T(8,128)(2,1)}, u32[]{:S(2)}) copy-start(bf16[2,64,768]{2,1,0:T(8,128)(2,1)} %copy-done.10) | copy-start | bytes 589828
  103.4 22.4 %collective-permute-start.26 = (bf16[3584,128]{1,0:T(8,128)(2,1)S(1)}, bf16[3584,128]{1,0:T(8,128)(2,1)S(1)}, u32[]{:S(2)}, u32[]{:S(2)}) collective-permute-start(bf16[3584,128]{1,0:T(8,128)(2,1)S(1)} %add_convert_fusion.1), channel_id=1, source_target_pairs={{0,4},{2,18},{4,8},{6,22},{8,12},{10,26},{12,0},{14,30},{16,20},{1... | collective-permute-start | bytes 2752520 | tf_op jit(solution)/shard_map/ppermute | solution.py:48
  105.2 20.7 %collective-permute-start.24 = (bf16[3584,128]{1,0:T(8,128)(2,1)S(1)}, bf16[3584,128]{1,0:T(8,128)(2,1)S(1)}, u32[]{:S(2)}, u32[]{:S(2)}) collective-permute-start(bf16[3584,128]{1,0:T(8,128)(2,1)S(1)} %add_convert_fusion.2), channel_id=1, source_target_pairs={{0,12},{2,50},{4,0},{6,54},{8,4},{10,58},{12,8},{14,62},{16,28},{1... | collective-permute-start | bytes 2752520 | tf_op jit(solution)/shard_map/ppermute | solution.py:48
  107.1 8.3 %collective-permute-start.30 = (bf16[128,768]{1,0:T(8,128)(2,1)S(1)}, bf16[128,768]{1,0:T(8,128)(2,1)S(1)}, u32[]{:S(2)}, u32[]{:S(2)}) collective-permute-start(bf16[128,768]{1,0:T(8,128)(2,1)S(1)} %bitcast.67), channel_id=1, source_target_pairs={{0,1},{1,0},{2,3},{3,2},{4,5},{5,4},{6,7},{7,6},{8,9},{9,8},{10,11... | collective-permute-start | bytes 589832 | tf_op jit(solution)/shard_map/ppermute | solution.py:387
  128.0 9.3 %collective-permute-start.31 = (bf16[2,448,128]{2,1,0:T(8,128)(2,1)S(1)}, bf16[2,448,128]{2,1,0:T(8,128)(2,1)S(1)}, u32[]{:S(2)}, u32[]{:S(2)}) collective-permute-start(bf16[2,448,128]{2,1,0:T(8,128)(2,1)S(1)} %get-tuple-element.72), channel_id=1, source_target_pairs={{0,48},{2,14},{4,52},{6,2},{8,56},{10,6},{12,60},{14,10},{16,0},{1... | collective-permute-start | bytes 688136 | tf_op jit(solution)/shard_map/ppermute | solution.py:48
  131.3 7.6 %collective-permute-start.32 = (bf16[2,448,128]{2,1,0:T(8,128)(2,1)S(1)}, bf16[2,448,128]{2,1,0:T(8,128)(2,1)S(1)}, u32[]{:S(2)}, u32[]{:S(2)}) collective-permute-start(bf16[2,448,128]{2,1,0:T(8,128)(2,1)S(1)} %get-tuple-element.73), channel_id=1, source_target_pairs={{0,32},{2,10},{4,36},{6,14},{8,40},{10,2},{12,44},{14,6},{16,48},{... | collective-permute-start | bytes 688136 | tf_op jit(solution)/shard_map/ppermute | solution.py:48
  131.3 9.7 %collective-permute-start.33 = (bf16[2,448,128]{2,1,0:T(8,128)(2,1)S(1)}, bf16[2,448,128]{2,1,0:T(8,128)(2,1)S(1)}, u32[]{:S(2)}, u32[]{:S(2)}) collective-permute-start(bf16[2,448,128]{2,1,0:T(8,128)(2,1)S(1)} %get-tuple-element.74), channel_id=1, source_target_pairs={{0,16},{2,6},{4,20},{6,10},{8,24},{10,14},{12,28},{14,2},{16,32},{... | collective-permute-start | bytes 688136 | tf_op jit(solution)/shard_map/ppermute | solution.py:48
  141.1 5.1 %collective-permute-start.34 = (bf16[448,128]{1,0:T(8,128)(2,1)S(1)}, bf16[448,128]{1,0:T(8,128)(2,1)S(1)}, u32[]{:S(2)}, u32[]{:S(2)}) collective-permute-start(bf16[448,128]{1,0:T(8,128)(2,1)S(1)} %fusion.3), channel_id=1, source_target_pairs={{0,64},{2,66},{4,68},{6,70},{8,72},{10,74},{12,76},{14,78},{16,80}... | collective-permute-start | bytes 344072 | tf_op jit(solution)/shard_map/ppermute | solution.py:48
  146.5 5.5 %collective-permute-start.35 = (bf16[144,128]{1,0:T(8,128)(2,1)S(1)}, bf16[144,128]{1,0:T(8,128)(2,1)S(1)}, u32[]{:S(2)}, u32[]{:S(2)}) collective-permute-start(bf16[144,128]{1,0:T(8,128)(2,1)S(1)} %get-tuple-element.81), channel_id=1, source_target_pairs={{0,1},{1,0},{2,3},{3,2},{4,5},{5,4},{6,7},{7,6},{8,9},{9,8},{10,11... | collective-permute-start | bytes 110600 | tf_op jit(solution)/shard_map/ppermute | solution.py:472
  (2 other events, 1.6 us)
